TPU v7x, 32 devices: a whole 2x2x4 slice. The times are simulated.
32 devices in a mesh: tm: 8 (over z, x), height: 4 (over y, core).
Axes of the slice: x: 2, y: 2, z: 4, core: 2. Of those that a mesh axis runs over, the one named last changes fastest.
Arguments:
- frames_in: bfloat16 [512, 128, 1024], P('tm', 'height'), may hold values from -6 to 6
- time_filter: bfloat16 [512, 64], replicated, may hold values from -0.25 to 0.25
- height_filter: bfloat16 [128, 64], replicated, may hold values from -0.5 to 0.5
Outputs:
- layer_out: bfloat16 [512, 128, 1024], P('tm', 'height')
All inputs are finite; a program needn't handle non-finite values.
Results may differ from a plain program's by a relative error of at most 0.0051.
Values may be sent and summed in bfloat16 or wider, within the bound.
No kernel may reach another device: no remote copies, remote signals or barrier semaphores. Data moves between devices by JAX's collectives and lax.ppermute only.
A program may use at most 128 MiB of HBM per device.

v0:
```python
import functools

import jax
import jax.numpy as jnp
import numpy as np
from jax import lax
from jax.experimental import pallas as pl
from jax.experimental.pallas import tpu as pltpu
from jax.sharding import PartitionSpec as P

F32, BF16 = jnp.float32, jnp.bfloat16
TILE = 128
WIDE = 2 * TILE
PARTS = 2
VMEM_BYTES = 62 << 20
FILTER_VMEM = 40 << 20
RUNS = 2
ANYWHERE = pl.BlockSpec(memory_space=pl.ANY)


def split_terms(table):
    high = table.astype(jnp.bfloat16)
    low = (table - high.astype(np.float64)).astype(jnp.bfloat16)
    return high, low


def fourier_tables(size):
    half = size // 2
    wave, at = np.arange(half)[:, None], np.arange(size)[None, :]
    angle = 2.0 * np.pi * ((wave * at) % size) / size
    sines = np.sin(angle)
    sines[0] = 1.0 - 2.0 * (np.arange(size) % 2)
    analysis = np.concatenate([np.cos(angle), sines], axis=0)
    weight = np.full((size,), 2.0 / size)
    weight[0] = weight[half] = 1.0 / size
    synthesis = (analysis * weight[:, None]).T
    return split_terms(analysis) + split_terms(synthesis)


def spectrum_kernel(taps_ref, high_ref, low_ref, out_ref):
    half = taps_ref.shape[0] // 2
    sums = jnp.dot(high_ref[...], taps_ref[...], preferred_element_type=F32)
    sums += jnp.dot(low_ref[...], taps_ref[...], preferred_element_type=F32)
    cosines, sines = sums[:half], sums[half:]
    first = lax.broadcasted_iota(jnp.int32, cosines.shape, 0) == 0
    out_ref[0] = cosines
    out_ref[1] = jnp.where(first, 0.0, sines)
    out_ref[2] = jnp.where(first, sines, cosines)


def filtered(signal, spectrum, tables):
    half = spectrum.shape[1]
    analysis_high, analysis_low, synthesis_high, synthesis_low = (t[...] for t in tables)
    coef = jnp.dot(analysis_high, signal, preferred_element_type=F32)
    coef += jnp.dot(analysis_low, signal, preferred_element_type=F32)
    cos_part, sin_part = coef[:half], coef[half:]
    keep, turn, other = (jnp.concatenate([spectrum[n]] * (signal.shape[1] // TILE), axis=1) for n in range(3))
    product = jnp.concatenate([cos_part * keep - sin_part * turn, sin_part * other + cos_part * turn], axis=0)
    high = product.astype(BF16)
    low = (product - high.astype(F32)).astype(BF16)
    result = jnp.dot(synthesis_high, high, preferred_element_type=F32)
    result += jnp.dot(synthesis_low, high, preferred_element_type=F32)
    result += jnp.dot(synthesis_high, low, preferred_element_type=F32)
    return result


class Cut:
    def __init__(self, frames, rows, width, tm, height):
        self.frames, self.rows, self.width, self.tm, self.height = frames, rows, width, tm, height
        self.devices = tm * height
        self.own = width // self.devices
        self.block = TILE // self.own
        self.frame_blocks, self.row_blocks = frames // self.block, rows // self.block
        self.tiles = width // TILE
        self.piece = (self.frame_blocks, rows, TILE)

    @staticmethod
    def fits(frames, rows, lanes, tm, height):
        own = lanes // PARTS // (tm * height)
        if own == 0 or TILE % own or lanes != PARTS * own * tm * height or lanes // PARTS % TILE:
            return False
        block = TILE // own
        return frames % block == 0 and rows % block == 0 and rows % 16 == 0 and rows // block % 2 == 0 and block % 8 == 0


def call(kernel, ins, outs, scratch=(), flops=0, held=None, dtype=BF16, vmem=VMEM_BYTES):
    unread = [] if held is None else [held]

    def body(*refs):
        kernel(*refs[: len(ins)], *refs[len(ins) + len(unread) :])

    moved = 2 * sum(int(np.prod(a.shape)) for a, _ in ins) + 2 * sum(int(np.prod(s)) for s, _ in outs)
    return pl.pallas_call(
        body,
        grid=(1,),
        in_specs=[spec for _, spec in ins] + [ANYWHERE] * len(unread),
        out_specs=[spec for _, spec in outs],
        out_shape=[jax.ShapeDtypeStruct(shape, dtype) for shape, _ in outs],
        scratch_shapes=list(scratch),
        input_output_aliases={} if held is None else {len(ins): 0},
        compiler_params=pltpu.CompilerParams(vmem_limit_bytes=vmem),
        cost_estimate=pl.CostEstimate(flops=flops, bytes_accessed=moved, transcendentals=0),
    )(*[array for array, _ in ins], *unread)


def whole(table):
    return table, pl.BlockSpec(table.shape, lambda n: (0,) * table.ndim)


def start_all(copies):
    for copy in copies:
        copy.start()
    return copies


def wait_all(copies):
    for copy in copies:
        copy.wait()


def load(pairs, sems, first=0):
    return start_all([pltpu.make_async_copy(a, b, sems.at[first + n]) for n, (a, b) in enumerate(pairs)])


def frame_runs(cut):
    step = cut.frames // steps_of(cut.frames, 16)
    return [pl.ds(first, step) for first in range(0, cut.frames, step)]


def fill_shuffle(cut, shuffle):
    shape = shuffle.shape
    row, column = (lax.broadcasted_iota(jnp.int32, shape, axis) for axis in range(2))
    m, n, lane = column // TILE, column % TILE // cut.own, column % cut.own
    shuffle[...] = (row == n * TILE + m * cut.own + lane).astype(F32).astype(BF16)


def shuffled(tiles, shuffle):
    moved = jnp.dot(jnp.concatenate(tiles, axis=1), shuffle[...], preferred_element_type=F32)
    return [moved[:, m * TILE : (m + 1) * TILE] for m in range(len(tiles))]


def in_turn(cut):
    count = next(n for n in (RUNS, 1) if cut.frame_blocks % n == 0)
    step = cut.frame_blocks // count
    return step, range(0, cut.frame_blocks, step), range(0, cut.block, 2)


def exchange_lanes(cut, step, lhs, shuffle, first):
    columns = slice(first * TILE, (first + 2) * TILE)
    moved = jnp.dot(lhs[...], shuffle[:, columns], preferred_element_type=F32)
    shape = (cut.tiles, step, cut.rows, TILE)
    return [(first + n, moved[:, n * TILE : (n + 1) * TILE].reshape(shape)) for n in range(2)]


def pack_kernel(lane, cut, x_ref, out_ref, x_buf, shuffle, lhs, out_buf, sems):
    step, runs, pairs = in_turn(cut)
    size = step * cut.rows
    frames = [pl.ds(run * cut.block, step * cut.block) for run in runs]
    arriving = load([(x_ref.at[at, :, pl.ds(lane, cut.width)], x_buf.at[at]) for at in frames], sems)
    fill_shuffle(cut, shuffle)
    leaving = []
    for turn, run in enumerate(runs):
        arriving[turn].wait()
        for tile in range(cut.tiles):
            lanes = slice(tile * TILE, (tile + 1) * TILE)
            x = x_buf[frames[turn], :, lanes].reshape(step, cut.block, cut.rows, TILE)
            for n in range(cut.block):
                lhs[tile * size : (tile + 1) * size, n * TILE : (n + 1) * TILE] = x[:, n].reshape(size, TILE)
        for pair in pairs:
            for m, piece in exchange_lanes(cut, step, lhs, shuffle, pair):
                for tile in range(cut.tiles):
                    out_buf[m * cut.tiles + tile, run : run + step] = piece[tile].astype(BF16)
            some = (pl.ds(pair * cut.tiles, 2 * cut.tiles), pl.ds(run, step))
            leaving += load([(out_buf.at[some], out_ref.at[some])], sems, len(runs) + len(leaving))
    wait_all(leaving)


def unpack_add_kernel(lane, cut, y_ref, x_ref, out_ref, y_buf, x_buf, shuffle, lhs, sems):
    step, runs, pairs = in_turn(cut)
    size = step * cut.rows
    lanes = pl.ds(lane, cut.width)
    parts = [pl.ds(run, step) for run in runs]
    frames = [pl.ds(run * cut.block, step * cut.block) for run in runs]
    arriving, added = [], []
    for turn, (part, at) in enumerate(zip(parts, frames)):
        arriving += load([(y_ref.at[:, part], y_buf.at[:, part])], sems, turn)
        added += load([(x_ref.at[at, :, lanes], x_buf.at[at])], sems, RUNS + turn)
    fill_shuffle(cut, shuffle)
    leaving = []
    for turn, run in enumerate(runs):
        arriving[turn].wait()
        for tile in range(cut.tiles):
            for m in range(cut.block):
                piece = y_buf[m * cut.tiles + tile, run : run + step].reshape(size, TILE)
                lhs[tile * size : (tile + 1) * size, m * TILE : (m + 1) * TILE] = piece
        added[turn].wait()
        for pair in pairs:
            for n, piece in exchange_lanes(cut, step, lhs, shuffle, pair):
                for tile in range(cut.tiles):
                    for block in range(step):
                        frame, at = (run + block) * cut.block + n, slice(tile * TILE, (tile + 1) * TILE)
                        x_buf[frame, :, at] = (x_buf[frame, :, at].astype(F32) + piece[tile, block]).astype(BF16)
        leaving += load([(x_buf.at[frames[turn]], out_ref.at[frames[turn], :, lanes])], sems, 2 * RUNS + turn)
    wait_all(leaving)


def filter_kernel(cut, x_ref, spectrum_ref, analysis_h, analysis_l, synthesis_h, synthesis_l, rows_ref, *refs):
    out_ref, x_buf, temporal, wide, column, spectrum, *tables, row_table, shuffle, sems = refs
    every = cut.height * cut.row_blocks
    frame_blocks = cut.tm * cut.frame_blocks
    arriving = load([(x_ref, x_buf), (spectrum_ref, spectrum)], sems)
    arriving += load(zip((analysis_h, analysis_l, synthesis_h, synthesis_l), tables), sems, 2)
    (rows_table,) = load([(rows_ref, row_table)], sems, 2 + len(tables))
    fill_shuffle(cut, shuffle)
    wait_all(arriving)

    def block_rows(n):
        return pl.ds(n, frame_blocks, stride=cut.rows)

    def block_frames(n):
        return pl.ds(n, frame_blocks, stride=cut.block)

    def along_time(j, _):
        for i in range(cut.tm):
            piece = x_buf[i * cut.height + j].astype(F32).reshape(-1, TILE)
            wide[i * piece.shape[0] : (i + 1) * piece.shape[0], :] = piece
        parts = [
            jnp.concatenate(
                [wide[block_rows(block * cut.block + n), :].astype(BF16) for block in range(cut.row_blocks)], axis=0
            )
            for n in range(cut.block)
        ]
        moved = shuffled(parts, shuffle)
        for block in range(cut.row_blocks):
            for n in range(cut.block):
                column[block, block_frames(n), :] = moved[n][block * frame_blocks : (block + 1) * frame_blocks]
        for block in range(0, cut.row_blocks, 2):
            signal = jnp.concatenate([column[block].astype(BF16), column[block + 1].astype(BF16)], axis=1)
            at = pl.ds(pl.multiple_of((j * cut.row_blocks + block) * TILE, WIDE), WIDE)
            temporal[:, at] = filtered(signal, spectrum[...], tables).astype(BF16)
        return _

    def along_rows(j, _):
        for block in range(0, cut.row_blocks, 2):
            first = pairs - 1 - (j * cut.row_blocks + block) // 2
            matrix = row_table[pl.ds(pl.multiple_of(first * WIDE, WIDE), pairs * WIDE), :]
            result = jnp.dot(temporal[...], matrix, preferred_element_type=F32)
            column[block], column[block + 1] = result[:, :TILE], result[:, TILE:]
        parts = [
            jnp.concatenate([column[block, block_frames(n), :].astype(BF16) for block in range(cut.row_blocks)], axis=0)
            for n in range(cut.block)
        ]
        moved = shuffled(parts, shuffle)
        for block in range(cut.row_blocks):
            for n in range(cut.block):
                rows = moved[n][block * frame_blocks : (block + 1) * frame_blocks]
                wide[block_rows(block * cut.block + n), :] = rows
        for i in range(cut.tm):
            count = cut.frame_blocks * cut.rows
            x_buf[i * cut.height + j] = wide[i * count : (i + 1) * count, :].astype(BF16).reshape(cut.piece)
        return _

    pairs = every // 2
    lax.fori_loop(0, cut.height, along_time, 0)
    rows_table.wait()
    lax.fori_loop(0, cut.height, along_rows, 0)
    wait_all(load([(x_buf, out_ref)], sems))


def row_matrices(cut, taps):
    size, own = taps.shape
    near = WIDE // own
    pairs = size // near
    far = np.arange(2 * pairs - 1)[:, None, None]
    source, target = np.arange(near)[None, :, None], np.arange(near)[None, None, :]
    index = ((2 * pairs - 1 - far - pairs) * near + target - source) % size
    chosen = (index.reshape(-1, 1) == np.arange(size)[None, :]).astype(jnp.bfloat16)
    picked = jnp.dot(chosen, taps, preferred_element_type=F32).astype(BF16)
    picked = picked.reshape((2 * pairs - 1) * near, 1, WIDE)
    same = jnp.asarray(np.tile(np.eye(own), (1, near)).astype(jnp.bfloat16))
    return (picked * same[None]).reshape((2 * pairs - 1) * WIDE, WIDE)


def shards(frames_in, time_taps, row_taps):
    frames, rows, lanes = frames_in.shape
    tm, height = lax.axis_size("tm"), lax.axis_size("height")
    if not Cut.fits(frames, rows, lanes, tm, height):
        return narrow_shards(frames_in, time_taps, row_taps)
    width = lanes // PARTS
    cut = Cut(frames, rows, width, tm, height)
    size = frames * tm
    tables = fourier_tables(size)
    device = lax.axis_index("tm") * height + lax.axis_index("height")

    def free(*arrays):
        return [(array, ANYWHERE) for array in arrays]

    shape = (cut.devices,) + cut.piece
    sems = pltpu.SemaphoreType.DMA((RUNS * (cut.block // 2 + 2) + 8,))
    part_buf, table_buf = pltpu.VMEM((frames, rows, width), BF16), pltpu.VMEM((cut.block * TILE,) * 2, BF16)
    piece_buf = pltpu.VMEM(shape, BF16)
    lhs = pltpu.VMEM((cut.tiles * in_turn(cut)[0] * rows, cut.block * TILE), BF16)

    def exchange(pieces):
        flat = pieces.reshape(cut.devices, -1, TILE)
        return lax.all_to_all(flat, ("tm", "height"), 0, 0, tiled=True).reshape(shape)

    def pack(part):
        kernel = functools.partial(pack_kernel, part * width, cut)
        scratch = [part_buf, table_buf, lhs, piece_buf, sems]
        return exchange(call(kernel, free(frames_in), free(shape), scratch)[0])

    def own_lanes(taps, part):
        first = (part * width + device % cut.tiles * TILE + device // cut.tiles * cut.own) % taps.shape[1]
        return lax.dynamic_slice_in_dim(taps, first, cut.own, axis=1)

    def both(pieces, part):
        taps = jnp.tile(own_lanes(time_taps, part), (1, TILE // cut.own))
        out = ((3, size // 2, TILE), pl.BlockSpec((3, size // 2, TILE), lambda n: (0, 0, 0)))
        (spectrum,) = call(spectrum_kernel, [whole(t) for t in (taps, *tables[:2])], [out], dtype=F32, vmem=FILTER_VMEM)
        matrices = row_matrices(cut, own_lanes(row_taps, part))
        every = rows * height * cut.own
        scratch = [piece_buf, pltpu.VMEM((size, every), BF16), pltpu.VMEM((size // cut.block * rows, TILE), F32)]
        scratch += [pltpu.VMEM((cut.row_blocks, size, TILE), F32), pltpu.VMEM(spectrum.shape, F32)]
        scratch += [pltpu.VMEM(t.shape, BF16) for t in (*tables, matrices)] + [table_buf, sems]
        ins = free(pieces, spectrum, *tables, matrices)
        flops = 2 * size * every * (5 * size + every)
        return exchange(call(functools.partial(filter_kernel, cut), ins, free(shape), scratch, flops, vmem=FILTER_VMEM)[0])

    def unpack_add(pieces, part, held):
        kernel = functools.partial(unpack_add_kernel, part * width, cut)
        scratch = [piece_buf, part_buf, table_buf, lhs, sems]
        return call(kernel, free(pieces, frames_in), free(frames_in.shape), scratch, held=held)[0]

    arrived = [pack(part) for part in range(PARTS)]
    returned = [both(pieces, part) for part, pieces in enumerate(arrived)]
    out = None
    for part, pieces in enumerate(returned):
        out = unpack_add(pieces, part, out)
    return out


def lane_taps(tap_table, first_lane, lane_count):
    channels = tap_table.shape[1]
    distinct = min(lane_count, channels)
    lane_ids = (first_lane + lax.iota(jnp.int32, distinct)) % channels
    selector = (lane_ids[None, :] == lax.iota(jnp.int32, channels)[:, None]).astype(tap_table.dtype)
    picked = jnp.dot(tap_table, selector, preferred_element_type=jnp.float32).astype(
        tap_table.dtype
    )
    return jnp.transpose(picked)


def shifted_taps(taps, base, size):
    distinct, period = taps.shape
    start = (base - (size - 1)) % period
    tiled = jnp.concatenate([taps, taps, taps], axis=1)
    window = lax.slice_in_dim(tiled, start, start + 2 * size - 1, axis=1)
    reversed_window = window[:, ::-1]
    padded = jnp.concatenate([reversed_window, jnp.zeros((distinct, 1), taps.dtype)], axis=1)
    repeated = jnp.tile(padded, (1, size + 1))
    flat = lax.slice_in_dim(repeated, size - 1, size - 1 + size * (2 * size - 1), axis=1)
    return flat.reshape(distinct, size, 2 * size - 1)[:, :, :size]


def time_convolve(segment, own_taps):
    frames, rows_here, lane_count = segment.shape
    distinct = own_taps.shape[0]
    columns = lane_count // distinct
    block_len = min(128, frames)
    block_count = frames // block_len
    blocked = segment.reshape(block_count, block_len, rows_here, columns, distinct)
    blocked = jnp.transpose(blocked, (4, 3, 2, 0, 1))
    running = jnp.zeros((distinct, columns, rows_here, block_count, block_len), jnp.float32)
    for lag_index in range(block_count):
        toeplitz = shifted_taps(own_taps, lag_index * block_len, block_len)
        rolled = jnp.roll(blocked, lag_index, axis=3)
        running = running + jnp.einsum(
            "cab,cxrnb->cxrna", toeplitz, rolled, preferred_element_type=jnp.float32
        )
    result = jnp.transpose(running, (3, 4, 2, 1, 0)).reshape(frames, rows_here, lane_count)
    return result.astype(jnp.bfloat16)


def row_convolve(segment, row_taps):
    frames, height, lane_count = segment.shape
    distinct = row_taps.shape[0]
    columns = lane_count // distinct
    arranged = jnp.transpose(segment.reshape(frames, height, columns, distinct), (3, 2, 0, 1))
    circulant = shifted_taps(row_taps, 0, height)
    filtered = jnp.einsum("cab,cxfb->cxfa", circulant, arranged, preferred_element_type=jnp.float32)
    result = jnp.transpose(filtered, (2, 3, 1, 0)).reshape(frames, height, lane_count)
    return result.astype(jnp.bfloat16)


def narrow_shards(frames_in, time_filter, height_filter):
    frames_dev, rows_dev, lane_total = frames_in.shape
    tm_count = lax.axis_size("tm")
    height_count = lax.axis_size("height")
    lane_count = lane_total // (tm_count * height_count)
    first_lane = (
        lax.axis_index("tm") * (lane_total // tm_count) + lax.axis_index("height") * lane_count
    )
    own_taps = lane_taps(time_filter, first_lane, lane_count)
    row_taps = lane_taps(height_filter, first_lane, lane_count)
    gathered = lax.all_to_all(
        lax.all_to_all(frames_in, "tm", split_axis=2, concat_axis=0, tiled=True),
        "height",
        split_axis=2,
        concat_axis=1,
        tiled=True,
    )
    temporal = time_convolve(gathered, own_taps)
    spatial_lanes = row_convolve(temporal, row_taps)
    returned = lax.all_to_all(
        lax.all_to_all(spatial_lanes, "tm", split_axis=0, concat_axis=2, tiled=True),
        "height",
        split_axis=1,
        concat_axis=2,
        tiled=True,
    )
    spatial = returned.reshape(frames_dev, rows_dev, height_count, tm_count, lane_count)
    spatial = jnp.transpose(spatial, (0, 1, 3, 2, 4)).reshape(frames_dev, rows_dev, lane_total)
    return (frames_in.astype(jnp.float32) + spatial.astype(jnp.float32)).astype(jnp.bfloat16)


def solution(mesh):
    return jax.shard_map(
        shards,
        mesh=mesh,
        in_specs=(P("tm", "height", None), P(), P()),
        out_specs=P("tm", "height", None),
        check_vma=False,
    )
```

profile of v0, /device:TPU:0, one launch (start us, length us, event | category | flops | bytes accessed | tf_op | source)
XLA Modules:
  0.0 225.6 jit_solution(2567825570639496622)
XLA Ops:
  0.0 4.8 %shard_map.112 = bf16[32,8,32,128]{3,2,1,0:T(8,128)(2,1)} custom-call(bf16[64,32,1024]{2,1,0:T(8,128)(2,1)} %refs_1_.5), custom_call_target="tpu_custom_call" | custom-call | bytes 6291456 | tf_op jit(solution)/shard_map/pallas_call | solution.py:93
  4.8 7.4 %all-to-all-start.2 = ((bf16[32,256,128]{2,1,0:T(8,128)(2,1)}), bf16[32,256,128]{2,1,0:T(8,128)(2,1)}, u32[]{:S(2)}, u32[]{:S(2)}) async-start(bf16[32,256,128]{2,1,0:T(8,128)(2,1)} %bitcast.21), calls=%async_computation.2 | async-start | bytes 4194304 | tf_op jit(solution)/shard_map/all_to_all | solution.py:306
  12.2 4.8 %shard_map.109 = bf16[32,8,32,128]{3,2,1,0:T(8,128)(2,1)} custom-call(bf16[64,32,1024]{2,1,0:T(8,128)(2,1)} %refs_1_.5), custom_call_target="tpu_custom_call" | custom-call | bytes 6291456 | tf_op jit(solution)/shard_map/pallas_call | solution.py:93
  17.0 44.0 %all-to-all-done.2 = bf16[32,256,128]{2,1,0:T(8,128)(2,1)} async-done(((bf16[32,256,128]{2,1,0:T(8,128)(2,1)}), bf16[32,256,128]{2,1,0:T(8,128)(2,1)}, u32[]{:S(2)}, u32[]{:S(2)}) %all-to-all-start.2) | async-done | bytes 2097184 | tf_op jit(solution)/shard_map/all_to_all | solution.py:306
  61.0 4.4 %all-to-all-start = ((bf16[32,256,128]{2,1,0:T(8,128)(2,1)}), bf16[32,256,128]{2,1,0:T(8,128)(2,1)}, u32[]{:S(2)}, u32[]{:S(2)}) async-start(bf16[32,256,128]{2,1,0:T(8,128)(2,1)} %bitcast.20), calls=%async_computation | async-start | bytes 4194304 | tf_op jit(solution)/shard_map/all_to_all | solution.py:306
  65.5 0.4 fusion.1
  65.9 0.5 copy.18
  66.4 0.9 mul.61
  67.6 0.5 copy.16
  68.1 0.9 mul.56
  69.2 0.4 shard_map.113.refs_1_
  70.0 0.7 copy-done.3
  70.9 27.9 %shard_map.114 = bf16[32,8,32,128]{3,2,1,0:T(8,128)(2,1)} custom-call(bf16[32,8,32,128]{3,2,1,0:T(8,128)(2,1)} %bitcast.8.refs_0_, f32[3,256,128]{2,1,0:T(8,128)S(1)} %shard_map.113.refs_1_, bf16[512,512]{1,0:T(8,128)(2,1)S(1)} %copy-done.1, bf16[512,512]{1,0:T(8,128)(2,1)S(1)} %copy-done.2, bf16[512,512]{1,0:T(8,128)(2,1)S(1)} %copy-done.3, ...), custom_call_target="tpu_custom_call" | custom-call | flops 9663676416 | bytes 8454144 | tf_op jit(solution)/shard_map/pallas_call | solution.py:93
  98.8 15.2 %all-to-all-done = bf16[32,256,128]{2,1,0:T(8,128)(2,1)} async-done(((bf16[32,256,128]{2,1,0:T(8,128)(2,1)}), bf16[32,256,128]{2,1,0:T(8,128)(2,1)}, u32[]{:S(2)}, u32[]{:S(2)}) %all-to-all-start) | async-done | bytes 2097184 | tf_op jit(solution)/shard_map/all_to_all | solution.py:306
  114.0 4.4 %all-to-all-start.3 = ((bf16[32,256,128]{2,1,0:T(8,128)(2,1)}), bf16[32,256,128]{2,1,0:T(8,128)(2,1)}, u32[]{:S(2)}, u32[]{:S(2)}) async-start(bf16[32,256,128]{2,1,0:T(8,128)(2,1)} %bitcast.12), calls=%async_computation.3 | async-start | bytes 4194304 | tf_op jit(solution)/shard_map/all_to_all | solution.py:306
  118.6 0.4 shard_map.110.refs_1_
  119.0 1.0 copy-done.4
  120.1 1.0 copy-done.6
  121.1 27.9 %shard_map.111 = bf16[32,8,32,128]{3,2,1,0:T(8,128)(2,1)} custom-call(bf16[32,8,32,128]{3,2,1,0:T(8,128)(2,1)} %bitcast.1.refs_0_, f32[3,256,128]{2,1,0:T(8,128)S(1)} %shard_map.110.refs_1_, bf16[512,512]{1,0:T(8,128)(2,1)S(1)} %copy-done.1, bf16[512,512]{1,0:T(8,128)(2,1)S(1)} %copy-done.2, bf16[512,512]{1,0:T(8,128)(2,1)S(1)} %copy-done.4, ...), custom_call_target="tpu_custom_call" | custom-call | flops 9663676416 | bytes 8454144 | tf_op jit(solution)/shard_map/pallas_call | solution.py:93
  149.0 17.9 %all-to-all-done.3 = bf16[32,256,128]{2,1,0:T(8,128)(2,1)} async-done(((bf16[32,256,128]{2,1,0:T(8,128)(2,1)}), bf16[32,256,128]{2,1,0:T(8,128)(2,1)}, u32[]{:S(2)}, u32[]{:S(2)}) %all-to-all-start.3) | async-done | bytes 2097184 | tf_op jit(solution)/shard_map/all_to_all | solution.py:306
  167.0 4.2 %all-to-all-start.1 = ((bf16[32,256,128]{2,1,0:T(8,128)(2,1)}), bf16[32,256,128]{2,1,0:T(8,128)(2,1)}, u32[]{:S(2)}, u32[]{:S(2)}) async-start(bf16[32,256,128]{2,1,0:T(8,128)(2,1)} %bitcast.5), calls=%async_computation.1 | async-start | bytes 4194304 | tf_op jit(solution)/shard_map/all_to_all | solution.py:306
  171.2 5.5 %shard_map.115.refs_2_ = bf16[64,32,1024]{2,1,0:T(8,128)(2,1)} custom-call(bf16[32,8,32,128]{3,2,1,0:T(8,128)(2,1)} %bitcast.13.refs_0_, bf16[64,32,1024]{2,1,0:T(8,128)(2,1)} %refs_1_.5), custom_call_target="tpu_custom_call" | custom-call | bytes 10485760 | tf_op jit(solution)/shard_map/pallas_call | solution.py:93
  176.7 43.3 %all-to-all-done.1 = bf16[32,256,128]{2,1,0:T(8,128)(2,1)} async-done(((bf16[32,256,128]{2,1,0:T(8,128)(2,1)}), bf16[32,256,128]{2,1,0:T(8,128)(2,1)}, u32[]{:S(2)}, u32[]{:S(2)}) %all-to-all-start.1) | async-done | bytes 2097184 | tf_op jit(solution)/shard_map/all_to_all | solution.py:306
  219.9 5.5 %shard_map.116 = bf16[64,32,1024]{2,1,0:T(8,128)(2,1)} custom-call(bf16[32,8,32,128]{3,2,1,0:T(8,128)(2,1)} %bitcast.6.refs_0_, bf16[64,32,1024]{2,1,0:T(8,128)(2,1)} %refs_1_.5, bf16[64,32,1024]{2,1,0:T(8,128)(2,1)} %shard_map.115.refs_2_), custom_call_target="tpu_custom_call", output_to_operand_aliasing={{}: (2, {})} | custom-call | bytes 10485760 | tf_op jit(solution)/shard_map/pallas_call | solution.py:93
  (24 shorter events, 1.2 us)
Async XLA Ops:
  0.0 65.5 %copy-start = (bf16[128,64]{0,1:T(8,128)(2,1)S(1)}, bf16[128,64]{0,1:T(8,128)(2,1)}, u32[]{:S(2)}) copy-start(bf16[128,64]{0,1:T(8,128)(2,1)} %param.13) | copy-start | bytes 49156
  4.8 56.2 %all-to-all-start.2 = ((bf16[32,256,128]{2,1,0:T(8,128)(2,1)}), bf16[32,256,128]{2,1,0:T(8,128)(2,1)}, u32[]{:S(2)}, u32[]{:S(2)}) async-start(bf16[32,256,128]{2,1,0:T(8,128)(2,1)} %bitcast.21), calls=%async_computation.2 | async-start | bytes 4194304 | tf_op jit(solution)/shard_map/all_to_all | solution.py:306
  61.0 4.5 %copy-start.7 = (bf16[3840,128]{1,0:T(8,128)(2,1)S(1)}, bf16[3840,128]{1,0:T(8,128)(2,1)}, u32[]{:S(2)}) copy-start(bf16[3840,128]{1,0:T(8,128)(2,1)} %constant.86.clone) | copy-start | bytes 2949124
  61.0 53.0 %all-to-all-start = ((bf16[32,256,128]{2,1,0:T(8,128)(2,1)}), bf16[32,256,128]{2,1,0:T(8,128)(2,1)}, u32[]{:S(2)}, u32[]{:S(2)}) async-start(bf16[32,256,128]{2,1,0:T(8,128)(2,1)} %bitcast.20), calls=%async_computation | async-start | bytes 4194304 | tf_op jit(solution)/shard_map/all_to_all | solution.py:306
  66.4 2.7 %copy-start.8 = (bf16[512,64]{0,1:T(8,128)(2,1)S(1)}, bf16[512,64]{0,1:T(8,128)(2,1)}, u32[]{:S(2)}) copy-start(bf16[512,64]{0,1:T(8,128)(2,1)} %param.12) | copy-start | bytes 196612
  67.2 2.0 copy-start.1
  67.3 2.0 copy-start.2
  67.6 2.0 copy-start.9
  69.7 1.0 copy-start.3
  69.7 1.2 copy-start.5
  114.0 53.0 %all-to-all-start.3 = ((bf16[32,256,128]{2,1,0:T(8,128)(2,1)}), bf16[32,256,128]{2,1,0:T(8,128)(2,1)}, u32[]{:S(2)}, u32[]{:S(2)}) async-start(bf16[32,256,128]{2,1,0:T(8,128)(2,1)} %bitcast.12), calls=%async_computation.3 | async-start | bytes 4194304 | tf_op jit(solution)/shard_map/all_to_all | solution.py:306
  119.0 1.0 copy-start.4
  120.1 1.0 copy-start.6
  167.0 53.0 %all-to-all-start.1 = ((bf16[32,256,128]{2,1,0:T(8,128)(2,1)}), bf16[32,256,128]{2,1,0:T(8,128)(2,1)}, u32[]{:S(2)}, u32[]{:S(2)}) async-start(bf16[32,256,128]{2,1,0:T(8,128)(2,1)} %bitcast.5), calls=%async_computation.1 | async-start | bytes 4194304 | tf_op jit(solution)/shard_map/all_to_all | solution.py:306
where the time goes:
time: 226 us
  waiting for transfers between devices  120 us (53%)
  Pallas kernels  77.2 us (34%)
  starting transfers between devices  20.5 us (9%)
  local copies, waits for them, and re-layouts  6 us (3%)
    all_to_all x4, waiting for transfers between devices, exchange(): lax.all_to_all(flat, ('tm', 'height'), 0, 0, tiled=True).reshape(shape)  120 us
    pallas_call x8, Pallas kernels, call(): pl.pallas_call(body, grid=(1,), in_specs=[spec for _, spec in ins] + [ANY...  77.2 us
    all_to_all x4, starting transfers between devices, exchange(): lax.all_to_all(flat, ('tm', 'height'), 0, 0, tiled=True).reshape(shape)  20.5 us
  transfers between devices with their start and end apart: 4, of which 4 were waited for; matrix products, arithmetic and copies ran while one was open for 2% of the time, Pallas kernels for 30%

commit v1 on v0

--- a/solution.py
+++ b/solution.py
@@ -15,6 +15,7 @@
 VMEM_BYTES = 62 << 20
 FILTER_VMEM = 40 << 20
 RUNS = 2
+FOLDS = 2
 ANYWHERE = pl.BlockSpec(memory_space=pl.ANY)
 
 
@@ -75,12 +76,12 @@
         self.piece = (self.frame_blocks, rows, TILE)
 
     @staticmethod
-    def fits(frames, rows, lanes, tm, height):
+    def fits(frames, rows, lanes, channels, tm, height):
         own = lanes // PARTS // (tm * height)
-        if own == 0 or TILE % own or lanes != PARTS * own * tm * height or lanes // PARTS % TILE:
+        if own == 0 or TILE % own or lanes != PARTS * own * tm * height or lanes // PARTS % TILE or channels % own:
             return False
         block = TILE // own
-        return frames % block == 0 and rows % block == 0 and rows % 16 == 0 and rows // block % 2 == 0 and block % 8 == 0
+        return frames % block == 0 and rows % block == 0 and rows % 16 == 0 and rows // block % 2 == 0 and block % (2 * FOLDS) == 0
 
 
 def call(kernel, ins, outs, scratch=(), flops=0, held=None, dtype=BF16, vmem=VMEM_BYTES):
@@ -131,12 +132,30 @@
     shape = shuffle.shape
     row, column = (lax.broadcasted_iota(jnp.int32, shape, axis) for axis in range(2))
     m, n, lane = column // TILE, column % TILE // cut.own, column % cut.own
-    shuffle[...] = (row == n * TILE + m * cut.own + lane).astype(F32).astype(BF16)
+    shuffle[...] = (row == n * (TILE // FOLDS) + m * cut.own + lane).astype(F32).astype(BF16)
+
+
+def folds(tiles):
+    for fold in range(FOLDS):
+        lanes = slice(fold * TILE // FOLDS, (fold + 1) * TILE // FOLDS)
+        yield [
+            jnp.concatenate([tile[:, lanes] for tile in tiles[n : n + FOLDS]], axis=1)
+            for n in range(0, len(tiles), FOLDS)
+        ]
 
 
 def shuffled(tiles, shuffle):
-    moved = jnp.dot(jnp.concatenate(tiles, axis=1), shuffle[...], preferred_element_type=F32)
-    return [moved[:, m * TILE : (m + 1) * TILE] for m in range(len(tiles))]
+    result = []
+    for part in folds(tiles):
+        moved = jnp.dot(jnp.concatenate(part, axis=1), shuffle[...], preferred_element_type=F32)
+        result += [moved[:, m * TILE : (m + 1) * TILE] for m in range(len(tiles) // FOLDS)]
+    return result
+
+
+def lay_out(tiles, lhs, rows):
+    for fold, part in enumerate(folds(tiles)):
+        for n, tile in enumerate(part):
+            lhs[fold, rows, n * TILE : (n + 1) * TILE] = tile
 
 
 def in_turn(cut):
@@ -146,8 +165,8 @@
 
 
 def exchange_lanes(cut, step, lhs, shuffle, first):
-    columns = slice(first * TILE, (first + 2) * TILE)
-    moved = jnp.dot(lhs[...], shuffle[:, columns], preferred_element_type=F32)
+    fold, at = divmod(first, cut.block // FOLDS)
+    moved = jnp.dot(lhs[fold], shuffle[:, at * TILE : (at + 2) * TILE], preferred_element_type=F32)
     shape = (cut.tiles, step, cut.rows, TILE)
     return [(first + n, moved[:, n * TILE : (n + 1) * TILE].reshape(shape)) for n in range(2)]
 
@@ -164,8 +183,7 @@
         for tile in range(cut.tiles):
             lanes = slice(tile * TILE, (tile + 1) * TILE)
             x = x_buf[frames[turn], :, lanes].reshape(step, cut.block, cut.rows, TILE)
-            for n in range(cut.block):
-                lhs[tile * size : (tile + 1) * size, n * TILE : (n + 1) * TILE] = x[:, n].reshape(size, TILE)
+            lay_out([x[:, n].reshape(size, TILE) for n in range(cut.block)], lhs, slice(tile * size, (tile + 1) * size))
         for pair in pairs:
             for m, piece in exchange_lanes(cut, step, lhs, shuffle, pair):
                 for tile in range(cut.tiles):
@@ -190,9 +208,8 @@
     for turn, run in enumerate(runs):
         arriving[turn].wait()
         for tile in range(cut.tiles):
-            for m in range(cut.block):
-                piece = y_buf[m * cut.tiles + tile, run : run + step].reshape(size, TILE)
-                lhs[tile * size : (tile + 1) * size, m * TILE : (m + 1) * TILE] = piece
+            y = [y_buf[m * cut.tiles + tile, run : run + step].reshape(size, TILE) for m in range(cut.block)]
+            lay_out(y, lhs, slice(tile * size, (tile + 1) * size))
         added[turn].wait()
         for pair in pairs:
             for n, piece in exchange_lanes(cut, step, lhs, shuffle, pair):
@@ -284,7 +301,7 @@
 def shards(frames_in, time_taps, row_taps):
     frames, rows, lanes = frames_in.shape
     tm, height = lax.axis_size("tm"), lax.axis_size("height")
-    if not Cut.fits(frames, rows, lanes, tm, height):
+    if not Cut.fits(frames, rows, lanes, time_taps.shape[1], tm, height):
         return narrow_shards(frames_in, time_taps, row_taps)
     width = lanes // PARTS
     cut = Cut(frames, rows, width, tm, height)
@@ -297,9 +314,9 @@
 
     shape = (cut.devices,) + cut.piece
     sems = pltpu.SemaphoreType.DMA((RUNS * (cut.block // 2 + 2) + 8,))
-    part_buf, table_buf = pltpu.VMEM((frames, rows, width), BF16), pltpu.VMEM((cut.block * TILE,) * 2, BF16)
+    part_buf, table_buf = pltpu.VMEM((frames, rows, width), BF16), pltpu.VMEM((cut.block * TILE // FOLDS,) * 2, BF16)
     piece_buf = pltpu.VMEM(shape, BF16)
-    lhs = pltpu.VMEM((cut.tiles * in_turn(cut)[0] * rows, cut.block * TILE), BF16)
+    lhs = pltpu.VMEM((FOLDS, cut.tiles * in_turn(cut)[0] * rows, cut.block * TILE // FOLDS), BF16)
 
     def exchange(pieces):
         flat = pieces.reshape(cut.devices, -1, TILE)

time: 226 us -> 224 us (level)
  Pallas kernels: 77.2 us -> 69.6 us
  waiting for transfers between devices: 120 us -> 126 us
    pallas_call x8, Pallas kernels: 77.2 us -> 69.6 us  [call(): pl.pallas_call(body, grid=(1,), in_specs=[spec for _, spec in ins] + [ANY...]
    all_to_all x4, waiting for transfers between devices: 120 us -> 126 us  [exchange(): lax.all_to_all(flat, ('tm', 'height'), 0, 0, tiled=True).reshape(shape)]
  transfers between devices with their start and end apart: 4 -> 4, of which waited for: 4 -> 4; matrix products, arithmetic and copies ran while one was open for 2% -> 2% of each run, Pallas kernels for 30% -> 27%
where the time goes in v1:
time: 224 us
  waiting for transfers between devices  126 us (56%)
  Pallas kernels  69.6 us (31%)
  starting transfers between devices  20.3 us (9%)
  local copies, waits for them, and re-layouts  6 us (3%)
    all_to_all x4, waiting for transfers between devices, exchange(): lax.all_to_all(flat, ('tm', 'height'), 0, 0, tiled=True).reshape(shape)  126 us
    pallas_call x8, Pallas kernels, call(): pl.pallas_call(body, grid=(1,), in_specs=[spec for _, spec in ins] + [ANY...  69.6 us
    all_to_all x4, starting transfers between devices, exchange(): lax.all_to_all(flat, ('tm', 'height'), 0, 0, tiled=True).reshape(shape)  20.3 us
  transfers between devices with their start and end apart: 4, of which 4 were waited for; matrix products, arithmetic and copies ran while one was open for 2% of the time, Pallas kernels for 27%

profile of v1, /device:TPU:0, one launch (start us, length us, event | category | flops | bytes accessed | tf_op | source)
XLA Modules:
  0.0 223.6 jit_solution(7931180484174318518)
XLA Ops:
  0.0 3.8 %shard_map.112 = bf16[32,8,32,128]{3,2,1,0:T(8,128)(2,1)} custom-call(bf16[64,32,1024]{2,1,0:T(8,128)(2,1)} %refs_1_.5), custom_call_target="tpu_custom_call" | custom-call | bytes 6291456 | tf_op jit(solution)/shard_map/pallas_call | solution.py:94
  3.9 7.4 %all-to-all-start.2 = ((bf16[32,256,128]{2,1,0:T(8,128)(2,1)}), bf16[32,256,128]{2,1,0:T(8,128)(2,1)}, u32[]{:S(2)}, u32[]{:S(2)}) async-start(bf16[32,256,128]{2,1,0:T(8,128)(2,1)} %bitcast.21), calls=%async_computation.2 | async-start | bytes 4194304 | tf_op jit(solution)/shard_map/all_to_all | solution.py:323
  11.3 3.8 %shard_map.109 = bf16[32,8,32,128]{3,2,1,0:T(8,128)(2,1)} custom-call(bf16[64,32,1024]{2,1,0:T(8,128)(2,1)} %refs_1_.5), custom_call_target="tpu_custom_call" | custom-call | bytes 6291456 | tf_op jit(solution)/shard_map/pallas_call | solution.py:94
  15.1 44.9 %all-to-all-done.2 = bf16[32,256,128]{2,1,0:T(8,128)(2,1)} async-done(((bf16[32,256,128]{2,1,0:T(8,128)(2,1)}), bf16[32,256,128]{2,1,0:T(8,128)(2,1)}, u32[]{:S(2)}, u32[]{:S(2)}) %all-to-all-start.2) | async-done | bytes 2097184 | tf_op jit(solution)/shard_map/all_to_all | solution.py:323
  60.0 4.2 %all-to-all-start = ((bf16[32,256,128]{2,1,0:T(8,128)(2,1)}), bf16[32,256,128]{2,1,0:T(8,128)(2,1)}, u32[]{:S(2)}, u32[]{:S(2)}) async-start(bf16[32,256,128]{2,1,0:T(8,128)(2,1)} %bitcast.20), calls=%async_computation | async-start | bytes 4194304 | tf_op jit(solution)/shard_map/all_to_all | solution.py:323
  64.4 0.4 fusion.1
  64.7 0.5 copy.18
  65.2 0.9 mul.61
  66.5 0.5 copy.16
  67.0 0.9 mul.56
  68.1 0.4 shard_map.113.refs_1_
  68.9 0.7 copy-done.3
  69.8 26.1 %shard_map.114 = bf16[32,8,32,128]{3,2,1,0:T(8,128)(2,1)} custom-call(bf16[32,8,32,128]{3,2,1,0:T(8,128)(2,1)} %bitcast.8.refs_0_, f32[3,256,128]{2,1,0:T(8,128)S(1)} %shard_map.113.refs_1_, bf16[512,512]{1,0:T(8,128)(2,1)S(1)} %copy-done.1, bf16[512,512]{1,0:T(8,128)(2,1)S(1)} %copy-done.2, bf16[512,512]{1,0:T(8,128)(2,1)S(1)} %copy-done.3, ...), custom_call_target="tpu_custom_call" | custom-call | flops 9663676416 | bytes 8454144 | tf_op jit(solution)/shard_map/pallas_call | solution.py:94
  95.8 17.2 %all-to-all-done = bf16[32,256,128]{2,1,0:T(8,128)(2,1)} async-done(((bf16[32,256,128]{2,1,0:T(8,128)(2,1)}), bf16[32,256,128]{2,1,0:T(8,128)(2,1)}, u32[]{:S(2)}, u32[]{:S(2)}) %all-to-all-start) | async-done | bytes 2097184 | tf_op jit(solution)/shard_map/all_to_all | solution.py:323
  113.0 4.4 %all-to-all-start.3 = ((bf16[32,256,128]{2,1,0:T(8,128)(2,1)}), bf16[32,256,128]{2,1,0:T(8,128)(2,1)}, u32[]{:S(2)}, u32[]{:S(2)}) async-start(bf16[32,256,128]{2,1,0:T(8,128)(2,1)} %bitcast.12), calls=%async_computation.3 | async-start | bytes 4194304 | tf_op jit(solution)/shard_map/all_to_all | solution.py:323
  117.6 0.4 shard_map.110.refs_1_
  118.0 1.0 copy-done.4
  119.1 1.0 copy-done.6
  120.1 26.1 %shard_map.111 = bf16[32,8,32,128]{3,2,1,0:T(8,128)(2,1)} custom-call(bf16[32,8,32,128]{3,2,1,0:T(8,128)(2,1)} %bitcast.1.refs_0_, f32[3,256,128]{2,1,0:T(8,128)S(1)} %shard_map.110.refs_1_, bf16[512,512]{1,0:T(8,128)(2,1)S(1)} %copy-done.1, bf16[512,512]{1,0:T(8,128)(2,1)S(1)} %copy-done.2, bf16[512,512]{1,0:T(8,128)(2,1)S(1)} %copy-done.4, ...), custom_call_target="tpu_custom_call" | custom-call | flops 9663676416 | bytes 8454144 | tf_op jit(solution)/shard_map/pallas_call | solution.py:94
  146.2 19.8 %all-to-all-done.3 = bf16[32,256,128]{2,1,0:T(8,128)(2,1)} async-done(((bf16[32,256,128]{2,1,0:T(8,128)(2,1)}), bf16[32,256,128]{2,1,0:T(8,128)(2,1)}, u32[]{:S(2)}, u32[]{:S(2)}) %all-to-all-start.3) | async-done | bytes 2097184 | tf_op jit(solution)/shard_map/all_to_all | solution.py:323
  166.0 4.2 %all-to-all-start.1 = ((bf16[32,256,128]{2,1,0:T(8,128)(2,1)}), bf16[32,256,128]{2,1,0:T(8,128)(2,1)}, u32[]{:S(2)}, u32[]{:S(2)}) async-start(bf16[32,256,128]{2,1,0:T(8,128)(2,1)} %bitcast.5), calls=%async_computation.1 | async-start | bytes 4194304 | tf_op jit(solution)/shard_map/all_to_all | solution.py:323
  170.3 4.5 %shard_map.115.refs_2_ = bf16[64,32,1024]{2,1,0:T(8,128)(2,1)} custom-call(bf16[32,8,32,128]{3,2,1,0:T(8,128)(2,1)} %bitcast.13.refs_0_, bf16[64,32,1024]{2,1,0:T(8,128)(2,1)} %refs_1_.5), custom_call_target="tpu_custom_call" | custom-call | bytes 10485760 | tf_op jit(solution)/shard_map/pallas_call | solution.py:94
  174.7 44.3 %all-to-all-done.1 = bf16[32,256,128]{2,1,0:T(8,128)(2,1)} async-done(((bf16[32,256,128]{2,1,0:T(8,128)(2,1)}), bf16[32,256,128]{2,1,0:T(8,128)(2,1)}, u32[]{:S(2)}, u32[]{:S(2)}) %all-to-all-start.1) | async-done | bytes 2097184 | tf_op jit(solution)/shard_map/all_to_all | solution.py:323
  219.0 4.5 %shard_map.116 = bf16[64,32,1024]{2,1,0:T(8,128)(2,1)} custom-call(bf16[32,8,32,128]{3,2,1,0:T(8,128)(2,1)} %bitcast.6.refs_0_, bf16[64,32,1024]{2,1,0:T(8,128)(2,1)} %refs_1_.5, bf16[64,32,1024]{2,1,0:T(8,128)(2,1)} %shard_map.115.refs_2_), custom_call_target="tpu_custom_call", output_to_operand_aliasing={{}: (2, {})} | custom-call | bytes 10485760 | tf_op jit(solution)/shard_map/pallas_call | solution.py:94
  (24 shorter events, 1.2 us)
Async XLA Ops:
  0.0 64.3 %copy-start = (bf16[128,64]{0,1:T(8,128)(2,1)S(1)}, bf16[128,64]{0,1:T(8,128)(2,1)}, u32[]{:S(2)}) copy-start(bf16[128,64]{0,1:T(8,128)(2,1)} %param.13) | copy-start | bytes 49156
  3.9 56.2 %all-to-all-start.2 = ((bf16[32,256,128]{2,1,0:T(8,128)(2,1)}), bf16[32,256,128]{2,1,0:T(8,128)(2,1)}, u32[]{:S(2)}, u32[]{:S(2)}) async-start(bf16[32,256,128]{2,1,0:T(8,128)(2,1)} %bitcast.21), calls=%async_computation.2 | async-start | bytes 4194304 | tf_op jit(solution)/shard_map/all_to_all | solution.py:323
  60.0 4.3 %copy-start.7 = (bf16[3840,128]{1,0:T(8,128)(2,1)S(1)}, bf16[3840,128]{1,0:T(8,128)(2,1)}, u32[]{:S(2)}) copy-start(bf16[3840,128]{1,0:T(8,128)(2,1)} %constant.86.clone) | copy-start | bytes 2949124
  60.0 53.0 %all-to-all-start = ((bf16[32,256,128]{2,1,0:T(8,128)(2,1)}), bf16[32,256,128]{2,1,0:T(8,128)(2,1)}, u32[]{:S(2)}, u32[]{:S(2)}) async-start(bf16[32,256,128]{2,1,0:T(8,128)(2,1)} %bitcast.20), calls=%async_computation | async-start | bytes 4194304 | tf_op jit(solution)/shard_map/all_to_all | solution.py:323
  65.2 2.7 %copy-start.8 = (bf16[512,64]{0,1:T(8,128)(2,1)S(1)}, bf16[512,64]{0,1:T(8,128)(2,1)}, u32[]{:S(2)}) copy-start(bf16[512,64]{0,1:T(8,128)(2,1)} %param.12) | copy-start | bytes 196612
  66.1 2.0 copy-start.1
  66.1 2.0 copy-start.2
  66.5 2.0 copy-start.9
  68.6 1.0 copy-start.3
  68.6 1.2 copy-start.5
  113.0 53.0 %all-to-all-start.3 = ((bf16[32,256,128]{2,1,0:T(8,128)(2,1)}), bf16[32,256,128]{2,1,0:T(8,128)(2,1)}, u32[]{:S(2)}, u32[]{:S(2)}) async-start(bf16[32,256,128]{2,1,0:T(8,128)(2,1)} %bitcast.12), calls=%async_computation.3 | async-start | bytes 4194304 | tf_op jit(solution)/shard_map/all_to_all | solution.py:323
  118.0 1.0 copy-start.4
  119.1 1.0 copy-start.6
  166.0 53.0 %all-to-all-start.1 = ((bf16[32,256,128]{2,1,0:T(8,128)(2,1)}), bf16[32,256,128]{2,1,0:T(8,128)(2,1)}, u32[]{:S(2)}, u32[]{:S(2)}) async-start(bf16[32,256,128]{2,1,0:T(8,128)(2,1)} %bitcast.5), calls=%async_computation.1 | async-start | bytes 4194304 | tf_op jit(solution)/shard_map/all_to_all | solution.py:323

commit v2 on v1

--- a/solution.py
+++ b/solution.py
@@ -12,10 +12,10 @@
 TILE = 128
 WIDE = 2 * TILE
 PARTS = 2
+RUNS = 2
+FOLDS = 2
 VMEM_BYTES = 62 << 20
 FILTER_VMEM = 40 << 20
-RUNS = 2
-FOLDS = 2
 ANYWHERE = pl.BlockSpec(memory_space=pl.ANY)
 
 
@@ -123,14 +123,9 @@
     return start_all([pltpu.make_async_copy(a, b, sems.at[first + n]) for n, (a, b) in enumerate(pairs)])
 
 
-def frame_runs(cut):
-    step = cut.frames // steps_of(cut.frames, 16)
-    return [pl.ds(first, step) for first in range(0, cut.frames, step)]
-
-
 def fill_shuffle(cut, shuffle):
-    shape = shuffle.shape
-    row, column = (lax.broadcasted_iota(jnp.int32, shape, axis) for axis in range(2))
+    row = lax.broadcasted_iota(jnp.int32, shuffle.shape, 0)
+    column = lax.broadcasted_iota(jnp.int32, (1, shuffle.shape[1]), 1)
     m, n, lane = column // TILE, column % TILE // cut.own, column % cut.own
     shuffle[...] = (row == n * (TILE // FOLDS) + m * cut.own + lane).astype(F32).astype(BF16)
 

time: 224 us -> 224 us (level)
  no operation moved by 1% of the time
where the time goes in v2:
time: 224 us
  waiting for transfers between devices  126 us (56%)
  Pallas kernels  69.6 us (31%)
  starting transfers between devices  20.3 us (9%)
  local copies, waits for them, and re-layouts  6 us (3%)
    all_to_all x4, waiting for transfers between devices, exchange(): lax.all_to_all(flat, ('tm', 'height'), 0, 0, tiled=True).reshape(shape)  126 us
    pallas_call x8, Pallas kernels, call(): pl.pallas_call(body, grid=(1,), in_specs=[spec for _, spec in ins] + [ANY...  69.6 us
    all_to_all x4, starting transfers between devices, exchange(): lax.all_to_all(flat, ('tm', 'height'), 0, 0, tiled=True).reshape(shape)  20.3 us
  transfers between devices with their start and end apart: 4, of which 4 were waited for; matrix products, arithmetic and copies ran while one was open for 2% of the time, Pallas kernels for 27%

profile of v2, /device:TPU:0, one launch (start us, length us, event | category | flops | bytes accessed | tf_op | source)
XLA Modules:
  0.0 223.6 jit_solution(7931180484174318518)
XLA Ops:
  0.0 3.8 %shard_map.112 = bf16[32,8,32,128]{3,2,1,0:T(8,128)(2,1)} custom-call(bf16[64,32,1024]{2,1,0:T(8,128)(2,1)} %refs_1_.5), custom_call_target="tpu_custom_call" | custom-call | bytes 6291456 | tf_op jit(solution)/shard_map/pallas_call | solution.py:94
  3.9 7.4 %all-to-all-start.2 = ((bf16[32,256,128]{2,1,0:T(8,128)(2,1)}), bf16[32,256,128]{2,1,0:T(8,128)(2,1)}, u32[]{:S(2)}, u32[]{:S(2)}) async-start(bf16[32,256,128]{2,1,0:T(8,128)(2,1)} %bitcast.21), calls=%async_computation.2 | async-start | bytes 4194304 | tf_op jit(solution)/shard_map/all_to_all | solution.py:318
  11.3 3.8 %shard_map.109 = bf16[32,8,32,128]{3,2,1,0:T(8,128)(2,1)} custom-call(bf16[64,32,1024]{2,1,0:T(8,128)(2,1)} %refs_1_.5), custom_call_target="tpu_custom_call" | custom-call | bytes 6291456 | tf_op jit(solution)/shard_map/pallas_call | solution.py:94
  15.1 44.9 %all-to-all-done.2 = bf16[32,256,128]{2,1,0:T(8,128)(2,1)} async-done(((bf16[32,256,128]{2,1,0:T(8,128)(2,1)}), bf16[32,256,128]{2,1,0:T(8,128)(2,1)}, u32[]{:S(2)}, u32[]{:S(2)}) %all-to-all-start.2) | async-done | bytes 2097184 | tf_op jit(solution)/shard_map/all_to_all | solution.py:318
  60.0 4.2 %all-to-all-start = ((bf16[32,256,128]{2,1,0:T(8,128)(2,1)}), bf16[32,256,128]{2,1,0:T(8,128)(2,1)}, u32[]{:S(2)}, u32[]{:S(2)}) async-start(bf16[32,256,128]{2,1,0:T(8,128)(2,1)} %bitcast.20), calls=%async_computation | async-start | bytes 4194304 | tf_op jit(solution)/shard_map/all_to_all | solution.py:318
  64.4 0.4 fusion.1
  64.7 0.5 copy.18
  65.2 0.9 mul.61
  66.5 0.5 copy.16
  67.0 0.9 mul.56
  68.1 0.4 shard_map.113.refs_1_
  68.9 0.7 copy-done.3
  69.8 26.1 %shard_map.114 = bf16[32,8,32,128]{3,2,1,0:T(8,128)(2,1)} custom-call(bf16[32,8,32,128]{3,2,1,0:T(8,128)(2,1)} %bitcast.8.refs_0_, f32[3,256,128]{2,1,0:T(8,128)S(1)} %shard_map.113.refs_1_, bf16[512,512]{1,0:T(8,128)(2,1)S(1)} %copy-done.1, bf16[512,512]{1,0:T(8,128)(2,1)S(1)} %copy-done.2, bf16[512,512]{1,0:T(8,128)(2,1)S(1)} %copy-done.3, ...), custom_call_target="tpu_custom_call" | custom-call | flops 9663676416 | bytes 8454144 | tf_op jit(solution)/shard_map/pallas_call | solution.py:94
  95.8 17.2 %all-to-all-done = bf16[32,256,128]{2,1,0:T(8,128)(2,1)} async-done(((bf16[32,256,128]{2,1,0:T(8,128)(2,1)}), bf16[32,256,128]{2,1,0:T(8,128)(2,1)}, u32[]{:S(2)}, u32[]{:S(2)}) %all-to-all-start) | async-done | bytes 2097184 | tf_op jit(solution)/shard_map/all_to_all | solution.py:318
  113.0 4.4 %all-to-all-start.3 = ((bf16[32,256,128]{2,1,0:T(8,128)(2,1)}), bf16[32,256,128]{2,1,0:T(8,128)(2,1)}, u32[]{:S(2)}, u32[]{:S(2)}) async-start(bf16[32,256,128]{2,1,0:T(8,128)(2,1)} %bitcast.12), calls=%async_computation.3 | async-start | bytes 4194304 | tf_op jit(solution)/shard_map/all_to_all | solution.py:318
  117.6 0.4 shard_map.110.refs_1_
  118.0 1.0 copy-done.4
  119.1 1.0 copy-done.6
  120.1 26.1 %shard_map.111 = bf16[32,8,32,128]{3,2,1,0:T(8,128)(2,1)} custom-call(bf16[32,8,32,128]{3,2,1,0:T(8,128)(2,1)} %bitcast.1.refs_0_, f32[3,256,128]{2,1,0:T(8,128)S(1)} %shard_map.110.refs_1_, bf16[512,512]{1,0:T(8,128)(2,1)S(1)} %copy-done.1, bf16[512,512]{1,0:T(8,128)(2,1)S(1)} %copy-done.2, bf16[512,512]{1,0:T(8,128)(2,1)S(1)} %copy-done.4, ...), custom_call_target="tpu_custom_call" | custom-call | flops 9663676416 | bytes 8454144 | tf_op jit(solution)/shard_map/pallas_call | solution.py:94
  146.2 19.8 %all-to-all-done.3 = bf16[32,256,128]{2,1,0:T(8,128)(2,1)} async-done(((bf16[32,256,128]{2,1,0:T(8,128)(2,1)}), bf16[32,256,128]{2,1,0:T(8,128)(2,1)}, u32[]{:S(2)}, u32[]{:S(2)}) %all-to-all-start.3) | async-done | bytes 2097184 | tf_op jit(solution)/shard_map/all_to_all | solution.py:318
  166.0 4.2 %all-to-all-start.1 = ((bf16[32,256,128]{2,1,0:T(8,128)(2,1)}), bf16[32,256,128]{2,1,0:T(8,128)(2,1)}, u32[]{:S(2)}, u32[]{:S(2)}) async-start(bf16[32,256,128]{2,1,0:T(8,128)(2,1)} %bitcast.5), calls=%async_computation.1 | async-start | bytes 4194304 | tf_op jit(solution)/shard_map/all_to_all | solution.py:318
  170.3 4.5 %shard_map.115.refs_2_ = bf16[64,32,1024]{2,1,0:T(8,128)(2,1)} custom-call(bf16[32,8,32,128]{3,2,1,0:T(8,128)(2,1)} %bitcast.13.refs_0_, bf16[64,32,1024]{2,1,0:T(8,128)(2,1)} %refs_1_.5), custom_call_target="tpu_custom_call" | custom-call | bytes 10485760 | tf_op jit(solution)/shard_map/pallas_call | solution.py:94
  174.7 44.3 %all-to-all-done.1 = bf16[32,256,128]{2,1,0:T(8,128)(2,1)} async-done(((bf16[32,256,128]{2,1,0:T(8,128)(2,1)}), bf16[32,256,128]{2,1,0:T(8,128)(2,1)}, u32[]{:S(2)}, u32[]{:S(2)}) %all-to-all-start.1) | async-done | bytes 2097184 | tf_op jit(solution)/shard_map/all_to_all | solution.py:318
  219.0 4.5 %shard_map.116 = bf16[64,32,1024]{2,1,0:T(8,128)(2,1)} custom-call(bf16[32,8,32,128]{3,2,1,0:T(8,128)(2,1)} %bitcast.6.refs_0_, bf16[64,32,1024]{2,1,0:T(8,128)(2,1)} %refs_1_.5, bf16[64,32,1024]{2,1,0:T(8,128)(2,1)} %shard_map.115.refs_2_), custom_call_target="tpu_custom_call", output_to_operand_aliasing={{}: (2, {})} | custom-call | bytes 10485760 | tf_op jit(solution)/shard_map/pallas_call | solution.py:94
  (24 shorter events, 1.2 us)
Async XLA Ops:
  0.0 64.3 %copy-start = (bf16[128,64]{0,1:T(8,128)(2,1)S(1)}, bf16[128,64]{0,1:T(8,128)(2,1)}, u32[]{:S(2)}) copy-start(bf16[128,64]{0,1:T(8,128)(2,1)} %param.13) | copy-start | bytes 49156
  3.9 56.2 %all-to-all-start.2 = ((bf16[32,256,128]{2,1,0:T(8,128)(2,1)}), bf16[32,256,128]{2,1,0:T(8,128)(2,1)}, u32[]{:S(2)}, u32[]{:S(2)}) async-start(bf16[32,256,128]{2,1,0:T(8,128)(2,1)} %bitcast.21), calls=%async_computation.2 | async-start | bytes 4194304 | tf_op jit(solution)/shard_map/all_to_all | solution.py:318
  60.0 4.3 %copy-start.7 = (bf16[3840,128]{1,0:T(8,128)(2,1)S(1)}, bf16[3840,128]{1,0:T(8,128)(2,1)}, u32[]{:S(2)}) copy-start(bf16[3840,128]{1,0:T(8,128)(2,1)} %constant.86.clone) | copy-start | bytes 2949124
  60.0 53.0 %all-to-all-start = ((bf16[32,256,128]{2,1,0:T(8,128)(2,1)}), bf16[32,256,128]{2,1,0:T(8,128)(2,1)}, u32[]{:S(2)}, u32[]{:S(2)}) async-start(bf16[32,256,128]{2,1,0:T(8,128)(2,1)} %bitcast.20), calls=%async_computation | async-start | bytes 4194304 | tf_op jit(solution)/shard_map/all_to_all | solution.py:318
  65.2 2.7 %copy-start.8 = (bf16[512,64]{0,1:T(8,128)(2,1)S(1)}, bf16[512,64]{0,1:T(8,128)(2,1)}, u32[]{:S(2)}) copy-start(bf16[512,64]{0,1:T(8,128)(2,1)} %param.12) | copy-start | bytes 196612
  66.1 2.0 copy-start.1
  66.1 2.0 copy-start.2
  66.5 2.0 copy-start.9
  68.6 1.0 copy-start.3
  68.6 1.2 copy-start.5
  113.0 53.0 %all-to-all-start.3 = ((bf16[32,256,128]{2,1,0:T(8,128)(2,1)}), bf16[32,256,128]{2,1,0:T(8,128)(2,1)}, u32[]{:S(2)}, u32[]{:S(2)}) async-start(bf16[32,256,128]{2,1,0:T(8,128)(2,1)} %bitcast.12), calls=%async_computation.3 | async-start | bytes 4194304 | tf_op jit(solution)/shard_map/all_to_all | solution.py:318
  118.0 1.0 copy-start.4
  119.1 1.0 copy-start.6
  166.0 53.0 %all-to-all-start.1 = ((bf16[32,256,128]{2,1,0:T(8,128)(2,1)}), bf16[32,256,128]{2,1,0:T(8,128)(2,1)}, u32[]{:S(2)}, u32[]{:S(2)}) async-start(bf16[32,256,128]{2,1,0:T(8,128)(2,1)} %bitcast.5), calls=%async_computation.1 | async-start | bytes 4194304 | tf_op jit(solution)/shard_map/all_to_all | solution.py:318

commit v3 on v2

--- a/solution.py
+++ b/solution.py
@@ -220,6 +220,7 @@
     out_ref, x_buf, temporal, wide, column, spectrum, *tables, row_table, shuffle, sems = refs
     every = cut.height * cut.row_blocks
     frame_blocks = cut.tm * cut.frame_blocks
+    size = cut.tm * cut.frames
     arriving = load([(x_ref, x_buf), (spectrum_ref, spectrum)], sems)
     arriving += load(zip((analysis_h, analysis_l, synthesis_h, synthesis_l), tables), sems, 2)
     (rows_table,) = load([(rows_ref, row_table)], sems, 2 + len(tables))
@@ -247,7 +248,7 @@
             for n in range(cut.block):
                 column[block, block_frames(n), :] = moved[n][block * frame_blocks : (block + 1) * frame_blocks]
         for block in range(0, cut.row_blocks, 2):
-            signal = jnp.concatenate([column[block].astype(BF16), column[block + 1].astype(BF16)], axis=1)
+            signal = jnp.concatenate([column[block + n, :size].astype(BF16) for n in range(2)], axis=1)
             at = pl.ds(pl.multiple_of((j * cut.row_blocks + block) * TILE, WIDE), WIDE)
             temporal[:, at] = filtered(signal, spectrum[...], tables).astype(BF16)
         return _
@@ -257,7 +258,7 @@
             first = pairs - 1 - (j * cut.row_blocks + block) // 2
             matrix = row_table[pl.ds(pl.multiple_of(first * WIDE, WIDE), pairs * WIDE), :]
             result = jnp.dot(temporal[...], matrix, preferred_element_type=F32)
-            column[block], column[block + 1] = result[:, :TILE], result[:, TILE:]
+            column[block, :size], column[block + 1, :size] = result[:, :TILE], result[:, TILE:]
         parts = [
             jnp.concatenate([column[block, block_frames(n), :].astype(BF16) for block in range(cut.row_blocks)], axis=0)
             for n in range(cut.block)
@@ -332,8 +333,8 @@
         (spectrum,) = call(spectrum_kernel, [whole(t) for t in (taps, *tables[:2])], [out], dtype=F32, vmem=FILTER_VMEM)
         matrices = row_matrices(cut, own_lanes(row_taps, part))
         every = rows * height * cut.own
-        scratch = [piece_buf, pltpu.VMEM((size, every), BF16), pltpu.VMEM((size // cut.block * rows, TILE), F32)]
-        scratch += [pltpu.VMEM((cut.row_blocks, size, TILE), F32), pltpu.VMEM(spectrum.shape, F32)]
+        scratch = [piece_buf, pltpu.VMEM((size, every), BF16), pltpu.VMEM(((size // cut.block + 1) * rows, TILE), F32)]
+        scratch += [pltpu.VMEM((cut.row_blocks, size + cut.block, TILE), F32), pltpu.VMEM(spectrum.shape, F32)]
         scratch += [pltpu.VMEM(t.shape, BF16) for t in (*tables, matrices)] + [table_buf, sems]
         ins = free(pieces, spectrum, *tables, matrices)
         flops = 2 * size * every * (5 * size + every)

time: 224 us -> 224 us (level)
  no operation moved by 1% of the time
where the time goes in v3:
time: 224 us
  waiting for transfers between devices  126 us (56%)
  Pallas kernels  69.6 us (31%)
  starting transfers between devices  20.3 us (9%)
  local copies, waits for them, and re-layouts  6 us (3%)
    all_to_all x4, waiting for transfers between devices, exchange(): lax.all_to_all(flat, ('tm', 'height'), 0, 0, tiled=True).reshape(shape)  126 us
    pallas_call x8, Pallas kernels, call(): pl.pallas_call(body, grid=(1,), in_specs=[spec for _, spec in ins] + [ANY...  69.6 us
    all_to_all x4, starting transfers between devices, exchange(): lax.all_to_all(flat, ('tm', 'height'), 0, 0, tiled=True).reshape(shape)  20.3 us
  transfers between devices with their start and end apart: 4, of which 4 were waited for; matrix products, arithmetic and copies ran while one was open for 2% of the time, Pallas kernels for 27%

profile of v3, /device:TPU:0, one launch (start us, length us, event | category | flops | bytes accessed | tf_op | source)
XLA Modules:
  0.0 223.6 jit_solution(18034065089989603607)
XLA Ops:
  0.0 3.8 %shard_map.112 = bf16[32,8,32,128]{3,2,1,0:T(8,128)(2,1)} custom-call(bf16[64,32,1024]{2,1,0:T(8,128)(2,1)} %refs_1_.5), custom_call_target="tpu_custom_call" | custom-call | bytes 6291456 | tf_op jit(solution)/shard_map/pallas_call | solution.py:94
  3.9 7.4 %all-to-all-start.2 = ((bf16[32,256,128]{2,1,0:T(8,128)(2,1)}), bf16[32,256,128]{2,1,0:T(8,128)(2,1)}, u32[]{:S(2)}, u32[]{:S(2)}) async-start(bf16[32,256,128]{2,1,0:T(8,128)(2,1)} %bitcast.21), calls=%async_computation.2 | async-start | bytes 4194304 | tf_op jit(solution)/shard_map/all_to_all | solution.py:319
  11.3 3.8 %shard_map.109 = bf16[32,8,32,128]{3,2,1,0:T(8,128)(2,1)} custom-call(bf16[64,32,1024]{2,1,0:T(8,128)(2,1)} %refs_1_.5), custom_call_target="tpu_custom_call" | custom-call | bytes 6291456 | tf_op jit(solution)/shard_map/pallas_call | solution.py:94
  15.1 44.9 %all-to-all-done.2 = bf16[32,256,128]{2,1,0:T(8,128)(2,1)} async-done(((bf16[32,256,128]{2,1,0:T(8,128)(2,1)}), bf16[32,256,128]{2,1,0:T(8,128)(2,1)}, u32[]{:S(2)}, u32[]{:S(2)}) %all-to-all-start.2) | async-done | bytes 2097184 | tf_op jit(solution)/shard_map/all_to_all | solution.py:319
  60.0 4.2 %all-to-all-start = ((bf16[32,256,128]{2,1,0:T(8,128)(2,1)}), bf16[32,256,128]{2,1,0:T(8,128)(2,1)}, u32[]{:S(2)}, u32[]{:S(2)}) async-start(bf16[32,256,128]{2,1,0:T(8,128)(2,1)} %bitcast.20), calls=%async_computation | async-start | bytes 4194304 | tf_op jit(solution)/shard_map/all_to_all | solution.py:319
  64.4 0.4 fusion.1
  64.7 0.5 copy.18
  65.2 0.9 mul.61
  66.5 0.5 copy.16
  67.0 0.9 mul.56
  68.1 0.4 shard_map.113.refs_1_
  68.9 0.7 copy-done.3
  69.8 26.1 %shard_map.114 = bf16[32,8,32,128]{3,2,1,0:T(8,128)(2,1)} custom-call(bf16[32,8,32,128]{3,2,1,0:T(8,128)(2,1)} %bitcast.8.refs_0_, f32[3,256,128]{2,1,0:T(8,128)S(1)} %shard_map.113.refs_1_, bf16[512,512]{1,0:T(8,128)(2,1)S(1)} %copy-done.1, bf16[512,512]{1,0:T(8,128)(2,1)S(1)} %copy-done.2, bf16[512,512]{1,0:T(8,128)(2,1)S(1)} %copy-done.3, ...), custom_call_target="tpu_custom_call" | custom-call | flops 9663676416 | bytes 8454144 | tf_op jit(solution)/shard_map/pallas_call | solution.py:94
  95.8 17.2 %all-to-all-done = bf16[32,256,128]{2,1,0:T(8,128)(2,1)} async-done(((bf16[32,256,128]{2,1,0:T(8,128)(2,1)}), bf16[32,256,128]{2,1,0:T(8,128)(2,1)}, u32[]{:S(2)}, u32[]{:S(2)}) %all-to-all-start) | async-done | bytes 2097184 | tf_op jit(solution)/shard_map/all_to_all | solution.py:319
  113.0 4.4 %all-to-all-start.3 = ((bf16[32,256,128]{2,1,0:T(8,128)(2,1)}), bf16[32,256,128]{2,1,0:T(8,128)(2,1)}, u32[]{:S(2)}, u32[]{:S(2)}) async-start(bf16[32,256,128]{2,1,0:T(8,128)(2,1)} %bitcast.12), calls=%async_computation.3 | async-start | bytes 4194304 | tf_op jit(solution)/shard_map/all_to_all | solution.py:319
  117.6 0.4 shard_map.110.refs_1_
  118.0 1.0 copy-done.4
  119.1 1.0 copy-done.6
  120.1 26.1 %shard_map.111 = bf16[32,8,32,128]{3,2,1,0:T(8,128)(2,1)} custom-call(bf16[32,8,32,128]{3,2,1,0:T(8,128)(2,1)} %bitcast.1.refs_0_, f32[3,256,128]{2,1,0:T(8,128)S(1)} %shard_map.110.refs_1_, bf16[512,512]{1,0:T(8,128)(2,1)S(1)} %copy-done.1, bf16[512,512]{1,0:T(8,128)(2,1)S(1)} %copy-done.2, bf16[512,512]{1,0:T(8,128)(2,1)S(1)} %copy-done.4, ...), custom_call_target="tpu_custom_call" | custom-call | flops 9663676416 | bytes 8454144 | tf_op jit(solution)/shard_map/pallas_call | solution.py:94
  146.2 19.8 %all-to-all-done.3 = bf16[32,256,128]{2,1,0:T(8,128)(2,1)} async-done(((bf16[32,256,128]{2,1,0:T(8,128)(2,1)}), bf16[32,256,128]{2,1,0:T(8,128)(2,1)}, u32[]{:S(2)}, u32[]{:S(2)}) %all-to-all-start.3) | async-done | bytes 2097184 | tf_op jit(solution)/shard_map/all_to_all | solution.py:319
  166.0 4.2 %all-to-all-start.1 = ((bf16[32,256,128]{2,1,0:T(8,128)(2,1)}), bf16[32,256,128]{2,1,0:T(8,128)(2,1)}, u32[]{:S(2)}, u32[]{:S(2)}) async-start(bf16[32,256,128]{2,1,0:T(8,128)(2,1)} %bitcast.5), calls=%async_computation.1 | async-start | bytes 4194304 | tf_op jit(solution)/shard_map/all_to_all | solution.py:319
  170.3 4.5 %shard_map.115.refs_2_ = bf16[64,32,1024]{2,1,0:T(8,128)(2,1)} custom-call(bf16[32,8,32,128]{3,2,1,0:T(8,128)(2,1)} %bitcast.13.refs_0_, bf16[64,32,1024]{2,1,0:T(8,128)(2,1)} %refs_1_.5), custom_call_target="tpu_custom_call" | custom-call | bytes 10485760 | tf_op jit(solution)/shard_map/pallas_call | solution.py:94
  174.7 44.3 %all-to-all-done.1 = bf16[32,256,128]{2,1,0:T(8,128)(2,1)} async-done(((bf16[32,256,128]{2,1,0:T(8,128)(2,1)}), bf16[32,256,128]{2,1,0:T(8,128)(2,1)}, u32[]{:S(2)}, u32[]{:S(2)}) %all-to-all-start.1) | async-done | bytes 2097184 | tf_op jit(solution)/shard_map/all_to_all | solution.py:319
  219.0 4.5 %shard_map.116 = bf16[64,32,1024]{2,1,0:T(8,128)(2,1)} custom-call(bf16[32,8,32,128]{3,2,1,0:T(8,128)(2,1)} %bitcast.6.refs_0_, bf16[64,32,1024]{2,1,0:T(8,128)(2,1)} %refs_1_.5, bf16[64,32,1024]{2,1,0:T(8,128)(2,1)} %shard_map.115.refs_2_), custom_call_target="tpu_custom_call", output_to_operand_aliasing={{}: (2, {})} | custom-call | bytes 10485760 | tf_op jit(solution)/shard_map/pallas_call | solution.py:94
  (24 shorter events, 1.2 us)
Async XLA Ops:
  0.0 64.3 %copy-start = (bf16[128,64]{0,1:T(8,128)(2,1)S(1)}, bf16[128,64]{0,1:T(8,128)(2,1)}, u32[]{:S(2)}) copy-start(bf16[128,64]{0,1:T(8,128)(2,1)} %param.13) | copy-start | bytes 49156
  3.9 56.2 %all-to-all-start.2 = ((bf16[32,256,128]{2,1,0:T(8,128)(2,1)}), bf16[32,256,128]{2,1,0:T(8,128)(2,1)}, u32[]{:S(2)}, u32[]{:S(2)}) async-start(bf16[32,256,128]{2,1,0:T(8,128)(2,1)} %bitcast.21), calls=%async_computation.2 | async-start | bytes 4194304 | tf_op jit(solution)/shard_map/all_to_all | solution.py:319
  60.0 4.3 %copy-start.7 = (bf16[3840,128]{1,0:T(8,128)(2,1)S(1)}, bf16[3840,128]{1,0:T(8,128)(2,1)}, u32[]{:S(2)}) copy-start(bf16[3840,128]{1,0:T(8,128)(2,1)} %constant.86.clone) | copy-start | bytes 2949124
  60.0 53.0 %all-to-all-start = ((bf16[32,256,128]{2,1,0:T(8,128)(2,1)}), bf16[32,256,128]{2,1,0:T(8,128)(2,1)}, u32[]{:S(2)}, u32[]{:S(2)}) async-start(bf16[32,256,128]{2,1,0:T(8,128)(2,1)} %bitcast.20), calls=%async_computation | async-start | bytes 4194304 | tf_op jit(solution)/shard_map/all_to_all | solution.py:319
  65.2 2.7 %copy-start.8 = (bf16[512,64]{0,1:T(8,128)(2,1)S(1)}, bf16[512,64]{0,1:T(8,128)(2,1)}, u32[]{:S(2)}) copy-start(bf16[512,64]{0,1:T(8,128)(2,1)} %param.12) | copy-start | bytes 196612
  66.1 2.0 copy-start.1
  66.1 2.0 copy-start.2
  66.5 2.0 copy-start.9
  68.6 1.0 copy-start.3
  68.6 1.2 copy-start.5
  113.0 53.0 %all-to-all-start.3 = ((bf16[32,256,128]{2,1,0:T(8,128)(2,1)}), bf16[32,256,128]{2,1,0:T(8,128)(2,1)}, u32[]{:S(2)}, u32[]{:S(2)}) async-start(bf16[32,256,128]{2,1,0:T(8,128)(2,1)} %bitcast.12), calls=%async_computation.3 | async-start | bytes 4194304 | tf_op jit(solution)/shard_map/all_to_all | solution.py:319
  118.0 1.0 copy-start.4
  119.1 1.0 copy-start.6
  166.0 53.0 %all-to-all-start.1 = ((bf16[32,256,128]{2,1,0:T(8,128)(2,1)}), bf16[32,256,128]{2,1,0:T(8,128)(2,1)}, u32[]{:S(2)}, u32[]{:S(2)}) async-start(bf16[32,256,128]{2,1,0:T(8,128)(2,1)} %bitcast.5), calls=%async_computation.1 | async-start | bytes 4194304 | tf_op jit(solution)/shard_map/all_to_all | solution.py:319

commit v4 on v3

--- a/solution.py
+++ b/solution.py
@@ -183,8 +183,10 @@
             for m, piece in exchange_lanes(cut, step, lhs, shuffle, pair):
                 for tile in range(cut.tiles):
                     out_buf[m * cut.tiles + tile, run : run + step] = piece[tile].astype(BF16)
-            some = (pl.ds(pair * cut.tiles, 2 * cut.tiles), pl.ds(run, step))
-            leaving += load([(out_buf.at[some], out_ref.at[some])], sems, len(runs) + len(leaving))
+            count = cut.block // FOLDS
+            if (pair + 2) % count == 0:
+                some = (pl.ds((pair + 2 - count) * cut.tiles, count * cut.tiles), pl.ds(run, step))
+                leaving += load([(out_buf.at[some], out_ref.at[some])], sems, len(runs) + len(leaving))
     wait_all(leaving)
 
 
@@ -309,7 +311,7 @@
         return [(array, ANYWHERE) for array in arrays]
 
     shape = (cut.devices,) + cut.piece
-    sems = pltpu.SemaphoreType.DMA((RUNS * (cut.block // 2 + 2) + 8,))
+    sems = pltpu.SemaphoreType.DMA((max(RUNS * (1 + FOLDS), 3 * RUNS, 7),))
     part_buf, table_buf = pltpu.VMEM((frames, rows, width), BF16), pltpu.VMEM((cut.block * TILE // FOLDS,) * 2, BF16)
     piece_buf = pltpu.VMEM(shape, BF16)
     lhs = pltpu.VMEM((FOLDS, cut.tiles * in_turn(cut)[0] * rows, cut.block * TILE // FOLDS), BF16)

time: 224 us -> 224 us (level)
  no operation moved by 1% of the time
where the time goes in v4:
time: 224 us; the launch traced here: 223 us
  waiting for transfers between devices  127 us (57%)
  Pallas kernels  68.8 us (31%)
  starting transfers between devices  20.3 us (9%)
  local copies, waits for them, and re-layouts  6 us (3%)
    all_to_all x4, waiting for transfers between devices, exchange(): lax.all_to_all(flat, ('tm', 'height'), 0, 0, tiled=True).reshape(shape)  127 us
    pallas_call x8, Pallas kernels, call(): pl.pallas_call(body, grid=(1,), in_specs=[spec for _, spec in ins] + [ANY...  68.8 us
    all_to_all x4, starting transfers between devices, exchange(): lax.all_to_all(flat, ('tm', 'height'), 0, 0, tiled=True).reshape(shape)  20.3 us
  transfers between devices with their start and end apart: 4, of which 4 were waited for; matrix products, arithmetic and copies ran while one was open for 2% of the time, Pallas kernels for 27%

profile of v4, /device:TPU:0, one launch (start us, length us, event | category | flops | bytes accessed | tf_op | source)
XLA Modules:
  0.0 223.3 jit_solution(14948448850076277275)
XLA Ops:
  0.0 3.6 %shard_map.112 = bf16[32,8,32,128]{3,2,1,0:T(8,128)(2,1)} custom-call(bf16[64,32,1024]{2,1,0:T(8,128)(2,1)} %refs_1_.5), custom_call_target="tpu_custom_call" | custom-call | bytes 6291456 | tf_op jit(solution)/shard_map/pallas_call | solution.py:94
  3.7 7.4 %all-to-all-start.2 = ((bf16[32,256,128]{2,1,0:T(8,128)(2,1)}), bf16[32,256,128]{2,1,0:T(8,128)(2,1)}, u32[]{:S(2)}, u32[]{:S(2)}) async-start(bf16[32,256,128]{2,1,0:T(8,128)(2,1)} %bitcast.21), calls=%async_computation.2 | async-start | bytes 4194304 | tf_op jit(solution)/shard_map/all_to_all | solution.py:321
  11.1 3.6 %shard_map.109 = bf16[32,8,32,128]{3,2,1,0:T(8,128)(2,1)} custom-call(bf16[64,32,1024]{2,1,0:T(8,128)(2,1)} %refs_1_.5), custom_call_target="tpu_custom_call" | custom-call | bytes 6291456 | tf_op jit(solution)/shard_map/pallas_call | solution.py:94
  14.7 45.1 %all-to-all-done.2 = bf16[32,256,128]{2,1,0:T(8,128)(2,1)} async-done(((bf16[32,256,128]{2,1,0:T(8,128)(2,1)}), bf16[32,256,128]{2,1,0:T(8,128)(2,1)}, u32[]{:S(2)}, u32[]{:S(2)}) %all-to-all-start.2) | async-done | bytes 2097184 | tf_op jit(solution)/shard_map/all_to_all | solution.py:321
  59.8 4.2 %all-to-all-start = ((bf16[32,256,128]{2,1,0:T(8,128)(2,1)}), bf16[32,256,128]{2,1,0:T(8,128)(2,1)}, u32[]{:S(2)}, u32[]{:S(2)}) async-start(bf16[32,256,128]{2,1,0:T(8,128)(2,1)} %bitcast.20), calls=%async_computation | async-start | bytes 4194304 | tf_op jit(solution)/shard_map/all_to_all | solution.py:321
  64.2 0.4 fusion.1
  64.5 0.5 copy.18
  65.0 0.9 mul.61
  66.3 0.5 copy.16
  66.8 0.9 mul.56
  67.9 0.4 shard_map.113.refs_1_
  68.7 0.7 copy-done.3
  69.6 26.0 %shard_map.114 = bf16[32,8,32,128]{3,2,1,0:T(8,128)(2,1)} custom-call(bf16[32,8,32,128]{3,2,1,0:T(8,128)(2,1)} %bitcast.8.refs_0_, f32[3,256,128]{2,1,0:T(8,128)S(1)} %shard_map.113.refs_1_, bf16[512,512]{1,0:T(8,128)(2,1)S(1)} %copy-done.1, bf16[512,512]{1,0:T(8,128)(2,1)S(1)} %copy-done.2, bf16[512,512]{1,0:T(8,128)(2,1)S(1)} %copy-done.3, ...), custom_call_target="tpu_custom_call" | custom-call | flops 9663676416 | bytes 8454144 | tf_op jit(solution)/shard_map/pallas_call | solution.py:94
  95.5 17.3 %all-to-all-done = bf16[32,256,128]{2,1,0:T(8,128)(2,1)} async-done(((bf16[32,256,128]{2,1,0:T(8,128)(2,1)}), bf16[32,256,128]{2,1,0:T(8,128)(2,1)}, u32[]{:S(2)}, u32[]{:S(2)}) %all-to-all-start) | async-done | bytes 2097184 | tf_op jit(solution)/shard_map/all_to_all | solution.py:321
  112.8 4.4 %all-to-all-start.3 = ((bf16[32,256,128]{2,1,0:T(8,128)(2,1)}), bf16[32,256,128]{2,1,0:T(8,128)(2,1)}, u32[]{:S(2)}, u32[]{:S(2)}) async-start(bf16[32,256,128]{2,1,0:T(8,128)(2,1)} %bitcast.12), calls=%async_computation.3 | async-start | bytes 4194304 | tf_op jit(solution)/shard_map/all_to_all | solution.py:321
  117.4 0.4 shard_map.110.refs_1_
  117.8 1.0 copy-done.4
  118.9 1.0 copy-done.6
  119.9 26.0 %shard_map.111 = bf16[32,8,32,128]{3,2,1,0:T(8,128)(2,1)} custom-call(bf16[32,8,32,128]{3,2,1,0:T(8,128)(2,1)} %bitcast.1.refs_0_, f32[3,256,128]{2,1,0:T(8,128)S(1)} %shard_map.110.refs_1_, bf16[512,512]{1,0:T(8,128)(2,1)S(1)} %copy-done.1, bf16[512,512]{1,0:T(8,128)(2,1)S(1)} %copy-done.2, bf16[512,512]{1,0:T(8,128)(2,1)S(1)} %copy-done.4, ...), custom_call_target="tpu_custom_call" | custom-call | flops 9663676416 | bytes 8454144 | tf_op jit(solution)/shard_map/pallas_call | solution.py:94
  145.9 19.9 %all-to-all-done.3 = bf16[32,256,128]{2,1,0:T(8,128)(2,1)} async-done(((bf16[32,256,128]{2,1,0:T(8,128)(2,1)}), bf16[32,256,128]{2,1,0:T(8,128)(2,1)}, u32[]{:S(2)}, u32[]{:S(2)}) %all-to-all-start.3) | async-done | bytes 2097184 | tf_op jit(solution)/shard_map/all_to_all | solution.py:321
  165.8 4.2 %all-to-all-start.1 = ((bf16[32,256,128]{2,1,0:T(8,128)(2,1)}), bf16[32,256,128]{2,1,0:T(8,128)(2,1)}, u32[]{:S(2)}, u32[]{:S(2)}) async-start(bf16[32,256,128]{2,1,0:T(8,128)(2,1)} %bitcast.5), calls=%async_computation.1 | async-start | bytes 4194304 | tf_op jit(solution)/shard_map/all_to_all | solution.py:321
  170.1 4.4 %shard_map.115.refs_2_ = bf16[64,32,1024]{2,1,0:T(8,128)(2,1)} custom-call(bf16[32,8,32,128]{3,2,1,0:T(8,128)(2,1)} %bitcast.13.refs_0_, bf16[64,32,1024]{2,1,0:T(8,128)(2,1)} %refs_1_.5), custom_call_target="tpu_custom_call" | custom-call | bytes 10485760 | tf_op jit(solution)/shard_map/pallas_call | solution.py:94
  174.4 44.4 %all-to-all-done.1 = bf16[32,256,128]{2,1,0:T(8,128)(2,1)} async-done(((bf16[32,256,128]{2,1,0:T(8,128)(2,1)}), bf16[32,256,128]{2,1,0:T(8,128)(2,1)}, u32[]{:S(2)}, u32[]{:S(2)}) %all-to-all-start.1) | async-done | bytes 2097184 | tf_op jit(solution)/shard_map/all_to_all | solution.py:321
  218.8 4.4 %shard_map.116 = bf16[64,32,1024]{2,1,0:T(8,128)(2,1)} custom-call(bf16[32,8,32,128]{3,2,1,0:T(8,128)(2,1)} %bitcast.6.refs_0_, bf16[64,32,1024]{2,1,0:T(8,128)(2,1)} %refs_1_.5, bf16[64,32,1024]{2,1,0:T(8,128)(2,1)} %shard_map.115.refs_2_), custom_call_target="tpu_custom_call", output_to_operand_aliasing={{}: (2, {})} | custom-call | bytes 10485760 | tf_op jit(solution)/shard_map/pallas_call | solution.py:94
  (24 shorter events, 1.2 us)
Async XLA Ops:
  0.0 64.1 %copy-start = (bf16[128,64]{0,1:T(8,128)(2,1)S(1)}, bf16[128,64]{0,1:T(8,128)(2,1)}, u32[]{:S(2)}) copy-start(bf16[128,64]{0,1:T(8,128)(2,1)} %param.13) | copy-start | bytes 49156
  3.7 56.2 %all-to-all-start.2 = ((bf16[32,256,128]{2,1,0:T(8,128)(2,1)}), bf16[32,256,128]{2,1,0:T(8,128)(2,1)}, u32[]{:S(2)}, u32[]{:S(2)}) async-start(bf16[32,256,128]{2,1,0:T(8,128)(2,1)} %bitcast.21), calls=%async_computation.2 | async-start | bytes 4194304 | tf_op jit(solution)/shard_map/all_to_all | solution.py:321
  59.8 4.3 %copy-start.7 = (bf16[3840,128]{1,0:T(8,128)(2,1)S(1)}, bf16[3840,128]{1,0:T(8,128)(2,1)}, u32[]{:S(2)}) copy-start(bf16[3840,128]{1,0:T(8,128)(2,1)} %constant.86.clone) | copy-start | bytes 2949124
  59.8 53.0 %all-to-all-start = ((bf16[32,256,128]{2,1,0:T(8,128)(2,1)}), bf16[32,256,128]{2,1,0:T(8,128)(2,1)}, u32[]{:S(2)}, u32[]{:S(2)}) async-start(bf16[32,256,128]{2,1,0:T(8,128)(2,1)} %bitcast.20), calls=%async_computation | async-start | bytes 4194304 | tf_op jit(solution)/shard_map/all_to_all | solution.py:321
  65.0 2.7 %copy-start.8 = (bf16[512,64]{0,1:T(8,128)(2,1)S(1)}, bf16[512,64]{0,1:T(8,128)(2,1)}, u32[]{:S(2)}) copy-start(bf16[512,64]{0,1:T(8,128)(2,1)} %param.12) | copy-start | bytes 196612
  65.9 2.0 copy-start.1
  65.9 2.0 copy-start.2
  66.3 2.0 copy-start.9
  68.4 1.0 copy-start.3
  68.4 1.2 copy-start.5
  112.8 53.0 %all-to-all-start.3 = ((bf16[32,256,128]{2,1,0:T(8,128)(2,1)}), bf16[32,256,128]{2,1,0:T(8,128)(2,1)}, u32[]{:S(2)}, u32[]{:S(2)}) async-start(bf16[32,256,128]{2,1,0:T(8,128)(2,1)} %bitcast.12), calls=%async_computation.3 | async-start | bytes 4194304 | tf_op jit(solution)/shard_map/all_to_all | solution.py:321
  117.8 1.0 copy-start.4
  118.9 1.0 copy-start.6
  165.8 53.0 %all-to-all-start.1 = ((bf16[32,256,128]{2,1,0:T(8,128)(2,1)}), bf16[32,256,128]{2,1,0:T(8,128)(2,1)}, u32[]{:S(2)}, u32[]{:S(2)}) async-start(bf16[32,256,128]{2,1,0:T(8,128)(2,1)} %bitcast.5), calls=%async_computation.1 | async-start | bytes 4194304 | tf_op jit(solution)/shard_map/all_to_all | solution.py:321

commit v5 on v4

--- a/solution.py
+++ b/solution.py
@@ -13,6 +13,7 @@
 WIDE = 2 * TILE
 PARTS = 2
 RUNS = 2
+EARLY = 4
 FOLDS = 2
 VMEM_BYTES = 62 << 20
 FILTER_VMEM = 40 << 20
@@ -154,26 +155,25 @@
 
 
 def in_turn(cut):
-    count = next(n for n in (RUNS, 1) if cut.frame_blocks % n == 0)
-    step = cut.frame_blocks // count
-    return step, range(0, cut.frame_blocks, step), range(0, cut.block, 2)
+    early = cut.frame_blocks // EARLY
+    return [run for run in ((0, early), (early, cut.frame_blocks - early)) if run[1]], range(0, cut.block, 2)
 
 
 def exchange_lanes(cut, step, lhs, shuffle, first):
     fold, at = divmod(first, cut.block // FOLDS)
-    moved = jnp.dot(lhs[fold], shuffle[:, at * TILE : (at + 2) * TILE], preferred_element_type=F32)
+    moved = jnp.dot(lhs[fold, : cut.tiles * step * cut.rows], shuffle[:, at * TILE : (at + 2) * TILE], preferred_element_type=F32)
     shape = (cut.tiles, step, cut.rows, TILE)
     return [(first + n, moved[:, n * TILE : (n + 1) * TILE].reshape(shape)) for n in range(2)]
 
 
 def pack_kernel(lane, cut, x_ref, out_ref, x_buf, shuffle, lhs, out_buf, sems):
-    step, runs, pairs = in_turn(cut)
-    size = step * cut.rows
-    frames = [pl.ds(run * cut.block, step * cut.block) for run in runs]
+    runs, pairs = in_turn(cut)
+    frames = [pl.ds(run * cut.block, step * cut.block) for run, step in runs]
     arriving = load([(x_ref.at[at, :, pl.ds(lane, cut.width)], x_buf.at[at]) for at in frames], sems)
     fill_shuffle(cut, shuffle)
     leaving = []
-    for turn, run in enumerate(runs):
+    for turn, (run, step) in enumerate(runs):
+        size = step * cut.rows
         arriving[turn].wait()
         for tile in range(cut.tiles):
             lanes = slice(tile * TILE, (tile + 1) * TILE)
@@ -191,18 +191,18 @@
 
 
 def unpack_add_kernel(lane, cut, y_ref, x_ref, out_ref, y_buf, x_buf, shuffle, lhs, sems):
-    step, runs, pairs = in_turn(cut)
-    size = step * cut.rows
+    runs, pairs = in_turn(cut)
     lanes = pl.ds(lane, cut.width)
-    parts = [pl.ds(run, step) for run in runs]
-    frames = [pl.ds(run * cut.block, step * cut.block) for run in runs]
+    parts = [pl.ds(run, step) for run, step in runs]
+    frames = [pl.ds(run * cut.block, step * cut.block) for run, step in runs]
     arriving, added = [], []
     for turn, (part, at) in enumerate(zip(parts, frames)):
         arriving += load([(y_ref.at[:, part], y_buf.at[:, part])], sems, turn)
         added += load([(x_ref.at[at, :, lanes], x_buf.at[at])], sems, RUNS + turn)
     fill_shuffle(cut, shuffle)
     leaving = []
-    for turn, run in enumerate(runs):
+    for turn, (run, step) in enumerate(runs):
+        size = step * cut.rows
         arriving[turn].wait()
         for tile in range(cut.tiles):
             y = [y_buf[m * cut.tiles + tile, run : run + step].reshape(size, TILE) for m in range(cut.block)]
@@ -314,7 +314,7 @@
     sems = pltpu.SemaphoreType.DMA((max(RUNS * (1 + FOLDS), 3 * RUNS, 7),))
     part_buf, table_buf = pltpu.VMEM((frames, rows, width), BF16), pltpu.VMEM((cut.block * TILE // FOLDS,) * 2, BF16)
     piece_buf = pltpu.VMEM(shape, BF16)
-    lhs = pltpu.VMEM((FOLDS, cut.tiles * in_turn(cut)[0] * rows, cut.block * TILE // FOLDS), BF16)
+    lhs = pltpu.VMEM((FOLDS, cut.tiles * max(n for _, n in in_turn(cut)[0]) * rows, cut.block * TILE // FOLDS), BF16)
 
     def exchange(pieces):
         flat = pieces.reshape(cut.devices, -1, TILE)

time: 224 us -> 224 us (level)
  no operation moved by 1% of the time
where the time goes in v5:
time: 224 us; the launch traced here: 223 us
  waiting for transfers between devices  127 us (57%)
  Pallas kernels  68.7 us (31%)
  starting transfers between devices  20.3 us (9%)
  local copies, waits for them, and re-layouts  6 us (3%)
    all_to_all x4, waiting for transfers between devices, exchange(): lax.all_to_all(flat, ('tm', 'height'), 0, 0, tiled=True).reshape(shape)  127 us
    pallas_call x8, Pallas kernels, call(): pl.pallas_call(body, grid=(1,), in_specs=[spec for _, spec in ins] + [ANY...  68.7 us
    all_to_all x4, starting transfers between devices, exchange(): lax.all_to_all(flat, ('tm', 'height'), 0, 0, tiled=True).reshape(shape)  20.3 us
  transfers between devices with their start and end apart: 4, of which 4 were waited for; matrix products, arithmetic and copies ran while one was open for 2% of the time, Pallas kernels for 27%

profile of v5, /device:TPU:0, one launch (start us, length us, event | category | flops | bytes accessed | tf_op | source)
XLA Modules:
  0.0 223.3 jit_solution(63970468349972357)
XLA Ops:
  0.0 3.6 %shard_map.112 = bf16[32,8,32,128]{3,2,1,0:T(8,128)(2,1)} custom-call(bf16[64,32,1024]{2,1,0:T(8,128)(2,1)} %refs_1_.5), custom_call_target="tpu_custom_call" | custom-call | bytes 6291456 | tf_op jit(solution)/shard_map/pallas_call | solution.py:95
  3.6 7.4 %all-to-all-start.2 = ((bf16[32,256,128]{2,1,0:T(8,128)(2,1)}), bf16[32,256,128]{2,1,0:T(8,128)(2,1)}, u32[]{:S(2)}, u32[]{:S(2)}) async-start(bf16[32,256,128]{2,1,0:T(8,128)(2,1)} %bitcast.21), calls=%async_computation.2 | async-start | bytes 4194304 | tf_op jit(solution)/shard_map/all_to_all | solution.py:321
  11.0 3.6 %shard_map.109 = bf16[32,8,32,128]{3,2,1,0:T(8,128)(2,1)} custom-call(bf16[64,32,1024]{2,1,0:T(8,128)(2,1)} %refs_1_.5), custom_call_target="tpu_custom_call" | custom-call | bytes 6291456 | tf_op jit(solution)/shard_map/pallas_call | solution.py:95
  14.6 45.2 %all-to-all-done.2 = bf16[32,256,128]{2,1,0:T(8,128)(2,1)} async-done(((bf16[32,256,128]{2,1,0:T(8,128)(2,1)}), bf16[32,256,128]{2,1,0:T(8,128)(2,1)}, u32[]{:S(2)}, u32[]{:S(2)}) %all-to-all-start.2) | async-done | bytes 2097184 | tf_op jit(solution)/shard_map/all_to_all | solution.py:321
  59.8 4.2 %all-to-all-start = ((bf16[32,256,128]{2,1,0:T(8,128)(2,1)}), bf16[32,256,128]{2,1,0:T(8,128)(2,1)}, u32[]{:S(2)}, u32[]{:S(2)}) async-start(bf16[32,256,128]{2,1,0:T(8,128)(2,1)} %bitcast.20), calls=%async_computation | async-start | bytes 4194304 | tf_op jit(solution)/shard_map/all_to_all | solution.py:321
  64.1 0.4 fusion.1
  64.5 0.5 copy.18
  65.0 0.9 mul.61
  66.3 0.5 copy.16
  66.8 0.9 mul.56
  67.9 0.4 shard_map.113.refs_1_
  68.7 0.7 copy-done.3
  69.5 26.0 %shard_map.114 = bf16[32,8,32,128]{3,2,1,0:T(8,128)(2,1)} custom-call(bf16[32,8,32,128]{3,2,1,0:T(8,128)(2,1)} %bitcast.8.refs_0_, f32[3,256,128]{2,1,0:T(8,128)S(1)} %shard_map.113.refs_1_, bf16[512,512]{1,0:T(8,128)(2,1)S(1)} %copy-done.1, bf16[512,512]{1,0:T(8,128)(2,1)S(1)} %copy-done.2, bf16[512,512]{1,0:T(8,128)(2,1)S(1)} %copy-done.3, ...), custom_call_target="tpu_custom_call" | custom-call | flops 9663676416 | bytes 8454144 | tf_op jit(solution)/shard_map/pallas_call | solution.py:95
  95.5 17.3 %all-to-all-done = bf16[32,256,128]{2,1,0:T(8,128)(2,1)} async-done(((bf16[32,256,128]{2,1,0:T(8,128)(2,1)}), bf16[32,256,128]{2,1,0:T(8,128)(2,1)}, u32[]{:S(2)}, u32[]{:S(2)}) %all-to-all-start) | async-done | bytes 2097184 | tf_op jit(solution)/shard_map/all_to_all | solution.py:321
  112.8 4.4 %all-to-all-start.3 = ((bf16[32,256,128]{2,1,0:T(8,128)(2,1)}), bf16[32,256,128]{2,1,0:T(8,128)(2,1)}, u32[]{:S(2)}, u32[]{:S(2)}) async-start(bf16[32,256,128]{2,1,0:T(8,128)(2,1)} %bitcast.12), calls=%async_computation.3 | async-start | bytes 4194304 | tf_op jit(solution)/shard_map/all_to_all | solution.py:321
  117.3 0.4 shard_map.110.refs_1_
  117.8 1.0 copy-done.4
  118.8 1.0 copy-done.6
  119.9 26.0 %shard_map.111 = bf16[32,8,32,128]{3,2,1,0:T(8,128)(2,1)} custom-call(bf16[32,8,32,128]{3,2,1,0:T(8,128)(2,1)} %bitcast.1.refs_0_, f32[3,256,128]{2,1,0:T(8,128)S(1)} %shard_map.110.refs_1_, bf16[512,512]{1,0:T(8,128)(2,1)S(1)} %copy-done.1, bf16[512,512]{1,0:T(8,128)(2,1)S(1)} %copy-done.2, bf16[512,512]{1,0:T(8,128)(2,1)S(1)} %copy-done.4, ...), custom_call_target="tpu_custom_call" | custom-call | flops 9663676416 | bytes 8454144 | tf_op jit(solution)/shard_map/pallas_call | solution.py:95
  145.8 19.9 %all-to-all-done.3 = bf16[32,256,128]{2,1,0:T(8,128)(2,1)} async-done(((bf16[32,256,128]{2,1,0:T(8,128)(2,1)}), bf16[32,256,128]{2,1,0:T(8,128)(2,1)}, u32[]{:S(2)}, u32[]{:S(2)}) %all-to-all-start.3) | async-done | bytes 2097184 | tf_op jit(solution)/shard_map/all_to_all | solution.py:321
  165.8 4.2 %all-to-all-start.1 = ((bf16[32,256,128]{2,1,0:T(8,128)(2,1)}), bf16[32,256,128]{2,1,0:T(8,128)(2,1)}, u32[]{:S(2)}, u32[]{:S(2)}) async-start(bf16[32,256,128]{2,1,0:T(8,128)(2,1)} %bitcast.5), calls=%async_computation.1 | async-start | bytes 4194304 | tf_op jit(solution)/shard_map/all_to_all | solution.py:321
  170.0 4.4 %shard_map.115.refs_2_ = bf16[64,32,1024]{2,1,0:T(8,128)(2,1)} custom-call(bf16[32,8,32,128]{3,2,1,0:T(8,128)(2,1)} %bitcast.13.refs_0_, bf16[64,32,1024]{2,1,0:T(8,128)(2,1)} %refs_1_.5), custom_call_target="tpu_custom_call" | custom-call | bytes 10485760 | tf_op jit(solution)/shard_map/pallas_call | solution.py:95
  174.4 44.3 %all-to-all-done.1 = bf16[32,256,128]{2,1,0:T(8,128)(2,1)} async-done(((bf16[32,256,128]{2,1,0:T(8,128)(2,1)}), bf16[32,256,128]{2,1,0:T(8,128)(2,1)}, u32[]{:S(2)}, u32[]{:S(2)}) %all-to-all-start.1) | async-done | bytes 2097184 | tf_op jit(solution)/shard_map/all_to_all | solution.py:321
  218.8 4.4 %shard_map.116 = bf16[64,32,1024]{2,1,0:T(8,128)(2,1)} custom-call(bf16[32,8,32,128]{3,2,1,0:T(8,128)(2,1)} %bitcast.6.refs_0_, bf16[64,32,1024]{2,1,0:T(8,128)(2,1)} %refs_1_.5, bf16[64,32,1024]{2,1,0:T(8,128)(2,1)} %shard_map.115.refs_2_), custom_call_target="tpu_custom_call", output_to_operand_aliasing={{}: (2, {})} | custom-call | bytes 10485760 | tf_op jit(solution)/shard_map/pallas_call | solution.py:95
  (24 shorter events, 1.2 us)
Async XLA Ops:
  0.0 64.1 %copy-start = (bf16[128,64]{0,1:T(8,128)(2,1)S(1)}, bf16[128,64]{0,1:T(8,128)(2,1)}, u32[]{:S(2)}) copy-start(bf16[128,64]{0,1:T(8,128)(2,1)} %param.13) | copy-start | bytes 49156
  3.6 56.2 %all-to-all-start.2 = ((bf16[32,256,128]{2,1,0:T(8,128)(2,1)}), bf16[32,256,128]{2,1,0:T(8,128)(2,1)}, u32[]{:S(2)}, u32[]{:S(2)}) async-start(bf16[32,256,128]{2,1,0:T(8,128)(2,1)} %bitcast.21), calls=%async_computation.2 | async-start | bytes 4194304 | tf_op jit(solution)/shard_map/all_to_all | solution.py:321
  59.8 4.3 %copy-start.7 = (bf16[3840,128]{1,0:T(8,128)(2,1)S(1)}, bf16[3840,128]{1,0:T(8,128)(2,1)}, u32[]{:S(2)}) copy-start(bf16[3840,128]{1,0:T(8,128)(2,1)} %constant.86.clone) | copy-start | bytes 2949124
  59.8 53.0 %all-to-all-start = ((bf16[32,256,128]{2,1,0:T(8,128)(2,1)}), bf16[32,256,128]{2,1,0:T(8,128)(2,1)}, u32[]{:S(2)}, u32[]{:S(2)}) async-start(bf16[32,256,128]{2,1,0:T(8,128)(2,1)} %bitcast.20), calls=%async_computation | async-start | bytes 4194304 | tf_op jit(solution)/shard_map/all_to_all | solution.py:321
  65.0 2.7 %copy-start.8 = (bf16[512,64]{0,1:T(8,128)(2,1)S(1)}, bf16[512,64]{0,1:T(8,128)(2,1)}, u32[]{:S(2)}) copy-start(bf16[512,64]{0,1:T(8,128)(2,1)} %param.12) | copy-start | bytes 196612
  65.9 2.0 copy-start.1
  65.9 2.0 copy-start.2
  66.3 2.0 copy-start.9
  68.3 1.0 copy-start.3
  68.3 1.2 copy-start.5
  112.8 53.0 %all-to-all-start.3 = ((bf16[32,256,128]{2,1,0:T(8,128)(2,1)}), bf16[32,256,128]{2,1,0:T(8,128)(2,1)}, u32[]{:S(2)}, u32[]{:S(2)}) async-start(bf16[32,256,128]{2,1,0:T(8,128)(2,1)} %bitcast.12), calls=%async_computation.3 | async-start | bytes 4194304 | tf_op jit(solution)/shard_map/all_to_all | solution.py:321
  117.8 1.0 copy-start.4
  118.8 1.0 copy-start.6
  165.8 53.0 %all-to-all-start.1 = ((bf16[32,256,128]{2,1,0:T(8,128)(2,1)}), bf16[32,256,128]{2,1,0:T(8,128)(2,1)}, u32[]{:S(2)}, u32[]{:S(2)}) async-start(bf16[32,256,128]{2,1,0:T(8,128)(2,1)} %bitcast.5), calls=%async_computation.1 | async-start | bytes 4194304 | tf_op jit(solution)/shard_map/all_to_all | solution.py:321
